TPU v7x, 512 devices: a whole 4x8x8 slice. The times are simulated.
512 devices in a mesh: feat: 16 (over y, core), node: 32 (over x, z).
Axes of the slice: x: 4, y: 8, z: 8, core: 2. Of those that a mesh axis runs over, the one named last changes fastest.
Arguments:
- features: bfloat16 [65536, 1024], P('node', 'feat'), may hold values from -6 to 6
- self_rows: int32 [32768], P('node'), may hold values from 0 to 2047
- neighbours: int32 [10, 32768], P(None, 'node'), may hold values from 0 to 65535, as said below
- w_self: bfloat16 [1024, 256], P('feat'), may hold values from -0.25 to 0.25
- w_neigh: bfloat16 [1024, 256], P('feat'), may hold values from -0.5 to 0.5
- cotangent: bfloat16 [32768, 256], P('node'), may hold values from -0.078125 to 0.078125
Outputs:
- hidden: bfloat16 [32768, 256], P(('node', 'feat'))
- grad_self: float32 [1024, 256], P('feat')
- grad_neigh: float32 [1024, 256], P('feat')
Inputs may be any that keep to these rules, and one draw needn't show every extreme that they name: `neighbours`: nodes p * 2048 to (p + 1) * 2048 - 1 belong to partition p. Among the 10240 entries of the targets of one partition, every partition is named exactly 3 * 1024 * 10 // 64 times (half of the partitions, the same half for every block) or exactly 1024 * 10 // 64 times (the others).
All inputs are finite; a program needn't handle non-finite values.
Results may differ from a plain program's by a relative error of at most 0.025.
Values may be sent and summed in bfloat16 or wider, within the bound.
A program may use at most 64 MiB of HBM per device.

v0:
```python
import jax
import jax.numpy as jnp
from jax import lax
from jax.sharding import PartitionSpec as P


def gelu_tanh(value):
    return jax.nn.gelu(value, approximate=True)


def on_device(features, self_rows, neighbours, w_self, w_neigh, cotangent):
    parts = lax.axis_size("node")
    nodes_dev = features.shape[0]
    t_dev = self_rows.shape[0]
    fanout = neighbours.shape[0]
    total = fanout * t_dev
    capacity = 3 * total // (2 * parts)
    flat = neighbours.reshape(-1)
    owner = flat // nodes_dev
    local = flat - owner * nodes_dev
    marks = (owner[:, None] == jnp.arange(parts, dtype=jnp.int32)[None, :]).astype(jnp.int32)
    before = jnp.cumsum(marks, axis=0) - marks
    slot = jnp.sum(before * marks, axis=1)
    place = owner * capacity + slot
    requests = (
        jnp.zeros((parts * capacity,), jnp.int32).at[place].set(local).reshape(parts, capacity)
    )
    wanted = lax.all_to_all(requests, "node", split_axis=0, concat_axis=0, tiled=True)
    returned = lax.all_to_all(features[wanted], "node", split_axis=0, concat_axis=0, tiled=True)
    fetched = returned.reshape(parts * capacity, -1)[place]
    neigh_mean = (
        jnp.sum(fetched.reshape(fanout, t_dev, -1), axis=0, dtype=jnp.float32) * (1.0 / fanout)
    ).astype(jnp.bfloat16)
    own = features[self_rows]
    share = t_dev // lax.axis_size("feat")
    first = lax.axis_index("feat") * share
    contract = (((0,), (0,)), ((), ()))
    own_part = own
    mean_part = neigh_mean
    pre = lax.psum_scatter(
        (
            jnp.dot(own_part, w_self, preferred_element_type=jnp.float32)
            + jnp.dot(mean_part, w_neigh, preferred_element_type=jnp.float32)
        ).astype(jnp.bfloat16),
        "feat",
        scatter_dimension=0,
        tiled=True,
    ).astype(jnp.float32)
    acts, backward = jax.vjp(gelu_tanh, pre)
    mine = lax.dynamic_slice_in_dim(cotangent, first, share).astype(jnp.float32)
    slope = backward(mine)[0].astype(jnp.bfloat16)
    hidden = acts.astype(jnp.bfloat16)
    piece = lax.all_gather(slope, "feat", axis=0, tiled=True)
    own_part = own
    mean_part = neigh_mean
    grad_self = lax.dot_general(own_part, piece, contract, preferred_element_type=jnp.float32)
    grad_neigh = lax.dot_general(mean_part, piece, contract, preferred_element_type=jnp.float32)
    grad_self, grad_neigh = (
        lax.psum(grad_self.astype(jnp.bfloat16), "node").astype(jnp.float32),
        lax.psum(grad_neigh.astype(jnp.bfloat16), "node").astype(jnp.float32),
    )
    return (hidden, grad_self, grad_neigh)


def solution(mesh):
    return jax.shard_map(
        on_device,
        mesh=mesh,
        in_specs=(
            P("node", "feat"),
            P("node"),
            P(None, "node"),
            P("feat", None),
            P("feat", None),
            P("node", None),
        ),
        out_specs=(P(("node", "feat"), None), P("feat", None), P("feat", None)),
        check_vma=False,
    )
```

profile of v0, /device:TPU:1, one launch (start us, length us, event | category | flops | bytes accessed | tf_op | source)
XLA Modules:
  0.0 463.1 jit_solution(10610092023099151848)
XLA Ops:
  7.2 0.9 reshape.171
  8.0 0.9 reshape.170
  9.0 9.7 %reduce-window.6 = s32[32,80,128]{2,1,0:T(8,128)S(1)} reduce-window(s32[32,80,128]{2,1,0:T(8,128)S(1)} %fusion.3, s32[]{:T(128)} %constant.20.clone.1), window={size=1x1x128 pad=0_0x0_0x127_0}, to_apply=%region_0.1 | reduce-window | flops 41615360 | bytes 2621444 | tf_op jit(solution)/shard_map/reduce-window
  18.8 1.0 slice_reduce_fusion
  21.7 38.0 %scatter_custom_fusion = s32[15360]{0:T(1024)S(1)} fusion(s32[10240]{0:T(1024)S(1)} %bitcast.42, s32[10240]{0:T(1024)S(1)} %get-tuple-element.5, s32[]{:T(128)} %constant.20.clone.1), kind=kCustom, calls=%fused_computation.59 | custom fusion | bytes 61444 | tf_op jit(solution)/shard_map/scatter | solution.py:26
  60.5 13.7 %all-to-all-start = ((s32[32,1,480]{2,1,0:T(1,128)}), s32[32,1,480]{2,1,0:T(1,128)S(1)}, u32[]{:S(2)}, u32[]{:S(2)}) async-start(s32[32,1,480]{2,1,0:T(1,128)} %all_to_all.11), calls=%async_computation | async-start | bytes 131072 | tf_op jit(solution)/shard_map/all_to_all | solution.py:28
  74.5 8.6 %all-to-all-done = s32[32,1,480]{2,1,0:T(1,128)S(1)} async-done(((s32[32,1,480]{2,1,0:T(1,128)}), s32[32,1,480]{2,1,0:T(1,128)S(1)}, u32[]{:S(2)}, u32[]{:S(2)}) %all-to-all-start) | async-done | bytes 61472 | tf_op jit(solution)/shard_map/all_to_all | solution.py:28
  83.4 53.9 %gather_fusion.1 = bf16[15360,64]{1,0:T(8,128)(2,1)} fusion(bf16[2048,64]{1,0:T(8,128)(2,1)S(1)} %copy.13, s32[15360]{0:T(1024)S(1)} %broadcast_clamp_fusion), kind=kCustom, calls=%fused_computation.1 | custom fusion | bytes 3993600 | tf_op jit(solution)/shard_map/gather | solution.py:29
  137.3 4.7 %copy.15 = bf16[32,480,64]{1,2,0:T(8,128)(2,1)} copy(bf16[32,480,64]{2,1,0:T(8,128)(2,1)} %bitcast.37) | data formatting | bytes 3932160 | tf_op jit(solution)/shard_map/gather | solution.py:29
  142.1 4.1 all-to-all-start.1
  146.3 3.2 gather_fusion
  149.5 1.2 fusion.26
  150.8 44.8 %all-to-all-done.1 = bf16[32,480,64]{1,2,0:T(8,128)(2,1)S(1)} async-done(((bf16[32,480,64]{1,2,0:T(8,128)(2,1)}), bf16[32,480,64]{1,2,0:T(8,128)(2,1)S(1)}, u32[]{:S(2)}, u32[]{:S(2)}) %all-to-all-start.1) | async-done | bytes 1966112 | tf_op jit(solution)/shard_map/all_to_all | solution.py:29
  195.6 3.1 copy.16
  198.7 30.0 %gather_fusion.2 = bf16[10240,64]{1,0:T(8,128)(2,1)S(1)} fusion(bf16[15360,64]{1,0:T(8,128)(2,1)} %bitcast.36, s32[10240]{0:T(1024)S(1)} %broadcast_clamp_fusion.1), kind=kCustom, calls=%fused_computation.2 | custom fusion | bytes 2662400 | tf_op jit(solution)/shard_map/gather | solution.py:30
  229.9 1.1 fusion.4
  231.0 55.9 %reduce-scatter.2.cloned.1.call-done = bf16[64,256]{1,0:T(8,128)(2,1)} async-done(((bf16[1024,256]{1,0:T(8,128)(2,1)}), bf16[64,256]{1,0:T(8,128)(2,1)}) %reduce-scatter.2.cloned.1.call-update) | async-done | bytes 32784 | tf_op jit(solution)/shard_map/reduce_scatter | solution.py:40
  286.9 1.4 fusion.8
  288.3 17.9 %all_gather.3 = bf16[1024,256]{1,0:T(8,128)(2,1)S(1)} all-gather(bf16[64,256]{1,0:T(8,128)(2,1)S(1)} %get-tuple-element.7), channel_id=1, replica_groups=mesh['feat'=16,'node'=32] {'feat'}, dimensions={0}, use_global_device_ids=true | all-gather | bytes 557056 | tf_op jit(solution)/shard_map/all_gather | solution.py:53
  306.2 0.9 convolution_convert_fusion
  307.1 0.9 convolution_convert_fusion.1
  308.0 145.4 %all-reduce.3.cloned.1.call-done = (bf16[64,256]{1,0:T(8,128)(2,1)}, bf16[64,256]{1,0:T(8,128)(2,1)}) async-done(((bf16[64,256]{1,0:T(8,128)(2,1)}, bf16[64,256]{1,0:T(8,128)(2,1)}), (bf16[64,256]{1,0:T(8,128)(2,1)}, bf16[64,256]{1,0:T(8,128)(2,1)})) %all-reduce.3.cloned.1.call-update) | async-done | bytes 65552 | tf_op jit(solution)/shard_map/psum | solution.py:59
  453.4 1.4 convert_element_type.54
  454.8 1.4 convert_element_type.56
  (32 shorter events, 4.8 us)
Async XLA Ops:
  7.2 142.4 %copy-start = (bf16[64,256]{1,0:T(8,128)(2,1)S(1)}, bf16[64,256]{1,0:T(8,128)(2,1)}, u32[]{:S(2)}) copy-start(bf16[64,256]{1,0:T(8,128)(2,1)} %param.9) | copy-start | bytes 98308
  20.0 0.8 copy-start.2
  20.5 53.7 %copy-start.3 = (bf16[2048,64]{0,1:T(8,128)(2,1)S(1)}, bf16[2048,64]{0,1:T(8,128)(2,1)}, u32[]{:S(2)}) copy-start(bf16[2048,64]{0,1:T(8,128)(2,1)} %param.6) | copy-start | bytes 786436
  60.5 22.6 %all-to-all-start = ((s32[32,1,480]{2,1,0:T(1,128)}), s32[32,1,480]{2,1,0:T(1,128)S(1)}, u32[]{:S(2)}, u32[]{:S(2)}) async-start(s32[32,1,480]{2,1,0:T(1,128)} %all_to_all.11), calls=%async_computation | async-start | bytes 131072 | tf_op jit(solution)/shard_map/all_to_all | solution.py:28
  142.1 4.2 copy-start.5
  142.1 53.5 %all-to-all-start.1 = ((bf16[32,480,64]{1,2,0:T(8,128)(2,1)}), bf16[32,480,64]{1,2,0:T(8,128)(2,1)S(1)}, u32[]{:S(2)}, u32[]{:S(2)}) async-start(bf16[32,480,64]{1,2,0:T(8,128)(2,1)} %copy.15), calls=%async_computation.1 | async-start | bytes 4194304 | tf_op jit(solution)/shard_map/all_to_all | solution.py:29
  146.2 140.6 %reduce-scatter.2.cloned.1.call-start = ((), (), s32[]{:S(2)}) async-start(), calls=%async_computation.3 | async-start | bytes 557056 | tf_op jit(solution)/shard_map/reduce_scatter | solution.py:40
  228.7 1.2 copy-start.1
  228.7 1.2 copy-start.4
  231.0 222.5 %all-reduce.3.cloned.1.call-start = ((), (), s32[]{:S(2)}) async-start(), calls=%async_computation.4 | async-start | bytes 131072 | tf_op jit(solution)/shard_map/psum | solution.py:59
Sparse Core Ops, SparseCore 0:
  231.1 55.7 reduce-scatter.1
  308.1 145.2 all-reduce.2
where the time goes:
time: 467 us; the launch traced here: 463 us
  waiting for transfers between devices  255 us (55%)
  local copies, waits for them, and re-layouts  138 us (30%)
  starting transfers between devices  17.9 us (4%)
  blocking collectives  17.9 us (4%)
  other arithmetic  16.5 us (4%)
  between operations  14.3 us (3%)
    psum x1, waiting for transfers between devices, on_device(): lax.psum(grad_self.astype(jnp.bfloat16), 'node').astype(jnp.float32)  145 us
    gather x2, local copies, waits for them, and re-layouts, on_device(): features[wanted]  58.7 us
    reduce_scatter x1, waiting for transfers between devices, on_device(): lax.psum_scatter((jnp.dot(own_part, w_self, preferred_element_type=jnp.fl...  55.9 us
    all_to_all x1, waiting for transfers between devices, on_device(): lax.all_to_all(features[wanted], 'node', split_axis=0, concat_axis=0, til...  44.8 us
    scatter x1, local copies, waits for them, and re-layouts, on_device(): jnp.zeros((parts * capacity,), jnp.int32).at[place].set(local)  38 us
    gather x1, local copies, waits for them, and re-layouts, on_device(): fetched = returned.reshape(parts * capacity, -1)[place]  30 us
    all_gather x1, blocking collectives, on_device(): piece = lax.all_gather(slope, 'feat', axis=0, tiled=True)  17.9 us
    all_to_all x1, starting transfers between devices, on_device(): lax.all_to_all(requests, 'node', split_axis=0, concat_axis=0, tiled=True)  13.7 us
  transfers between devices with their start and end apart: 4, of which 4 were waited for; matrix products, arithmetic and copies ran while one was open for 1% of the time, Pallas kernels for 0%

commit v1 on v0

v1 whole, which is shorter than its diff:
```python
import functools
import math

import jax
import jax.numpy as jnp
from jax import lax
from jax.experimental import pallas as pl
from jax.experimental.pallas import tpu as pltpu
from jax.sharding import PartitionSpec as P

NX, NZ, NY = 4, 8, 8
NODES = NX * NZ
FAN = 10
ROWS = 2048
HALF = ROWS // 2
QUART = HALF // 2
COLS = 64
WIDE = 2 * COLS
HID = 256
SHARE = 64
TGT = NY * SHARE
GROUP = 2 * NX
NZG = NZ // 2
TAB = GROUP * ROWS
MESH = pl.DeviceIdType.MESH
VM = 56 * 2**20

SORT10 = (
    ((0, 8), (1, 9), (2, 7), (3, 5), (4, 6)),
    ((0, 2), (1, 4), (5, 8), (7, 9)),
    ((0, 3), (2, 4), (5, 7), (6, 9)),
    ((0, 1), (3, 6), (8, 9)),
    ((1, 5), (2, 3), (4, 8), (6, 7)),
    ((1, 2), (3, 5), (4, 6), (7, 8)),
    ((2, 3), (4, 5), (6, 7)),
    ((3, 4), (5, 6)),
)


def where_am_i():
    feat, node = lax.axis_index("feat"), lax.axis_index("node")
    return feat // 2, feat % 2, node // NZ, node % NZ


def dev(y, c, x, z):
    return {"feat": y * 2 + c, "node": x * NZ + z}


def remote(src, dst, send, recv, to):
    return pltpu.make_async_remote_copy(
        src_ref=src, dst_ref=dst, send_sem=send, recv_sem=recv, device_id=to, device_id_type=MESH
    )


def gather_kernel(feat, nb, ws, wn, tab, idx, cnt, wf, other, nbs, s_x, r_x, s_t, r_t, s_n, r_n, s_w, r_w, s_f, r_f):
    y, c, x, z = where_am_i()
    zl, zh = z % 2, z // 2
    xr, xl, zp = (x + 1) % NX, (x + NX - 1) % NX, z + 1 - 2 * zl
    right, left, over = dev(y, c, xr, z), dev(y, c, xl, z), dev(y, c, x, zp)
    partner = dev(y, 1 - c, x, z)
    barrier = pltpu.get_barrier_semaphore()
    for to in (right, left, over, partner):
        pl.semaphore_signal(barrier, inc=1, device_id=to, device_id_type=MESH)
    for d in range(1, NZG):
        pl.semaphore_signal(barrier, inc=1, device_id=dev(y, c, x, (z + 2 * d) % NZ), device_id_type=MESH)
    for d in range(1, NY):
        pl.semaphore_signal(barrier, inc=1, device_id=dev((y + d) % NY, c, x, z), device_id_type=MESH)

    k = y * 2 + c
    wf[k, 0] = ws[...]
    wf[k, 1] = wn[...]
    mine = []
    for b in range(NY):
        lo = nb[:, b * 128 : b * 128 + 64]
        hi = nb[:, b * 128 + 64 : b * 128 + 128]
        mine.append(jnp.where(c == 0, lo, hi))
    nbs[zh] = jnp.concatenate(mine, axis=1)

    pl.semaphore_wait(barrier, 4 + (NZG - 1) + (NY - 1))

    give = pl.multiple_of((1 - c) * HALF, HALF)
    keep = pl.multiple_of(c * HALF, HALF)
    swap = remote(feat.at[pl.ds(give, HALF)], other, s_x, r_x, partner)
    swap.start()
    for d in range(1, NZG):
        remote(nbs.at[zh], nbs.at[zh], s_n.at[d], r_n.at[d], dev(y, c, x, (z + 2 * d) % NZ)).start()
    for d in range(1, NY):
        remote(wf.at[k], wf.at[k], s_w.at[d], r_w.at[d], dev((y + d) % NY, c, x, z)).start()
    remote(wf.at[k], wf.at[k], s_f.at[0], r_f.at[0], partner).start()
    swap.wait_recv()
    own = x * 2 + zl

    def widen(i, _):
        at = pl.multiple_of(i * 128, 128)
        a = feat[pl.ds(keep + at, 128), :]
        b = other[pl.ds(at, 128), :]
        tab[own, c, pl.ds(at, 128), :] = jnp.where(
            c == 0, jnp.concatenate([a, b], axis=1), jnp.concatenate([b, a], axis=1)
        )
        return 0

    lax.fori_loop(0, HALF // 128, widen, 0)

    slot = lambda i, zz: i * 2 + zz
    zo = 1 - zl
    whole = lambda i, zz: tab.at[slot(i, zz), c]
    part = lambda i, zz, h: tab.at[slot(i, zz), c, pl.ds(h * QUART, QUART)]
    far = (x + 2) % NX
    sends = []

    def go(m, ref, to):
        copy = remote(ref, ref, s_t.at[m], r_t.at[m], to)
        copy.start()
        sends.append(copy)

    def come(m, ref):
        remote(ref, ref, s_t.at[m], r_t.at[m], partner).wait_recv()

    go(0, whole(x, zl), right)
    go(1, whole(x, zl), left)
    go(2, whole(x, zl), over)
    go(9, whole(x, zl), partner)
    come(0, whole(xl, zl))
    go(3, part(xl, zl, 0), right)
    go(10, whole(xl, zl), partner)
    come(1, whole(xr, zl))
    go(4, part(xr, zl, 1), left)
    go(11, whole(xr, zl), partner)
    come(2, whole(x, zo))
    go(5, whole(x, zo), right)
    go(6, whole(x, zo), left)
    go(12, whole(x, zo), partner)
    come(3, part(far, zl, 0))
    go(7, part(far, zl, 0), over)
    go(13, part(far, zl, 0), partner)
    come(4, part(far, zl, 1))
    go(8, part(far, zl, 1), over)
    go(14, part(far, zl, 1), partner)

    for d in range(1, NZG):
        at = (zh + NZG - d) % NZG
        remote(nbs.at[at], nbs.at[at], s_n.at[d], r_n.at[d], partner).wait_recv()
    wires = []
    for f in range(FAN):
        n = jnp.concatenate([nbs[g, f : f + 1, :] for g in range(NZG)], axis=0)
        part_of = n >> 11
        inside = ((part_of & 7) >> 1) == zh
        row = ((((part_of >> 3) << 1) | (part_of & 1)) << 11) | (n & (ROWS - 1))
        wires.append(jnp.where(inside, row, TAB))
    for layer in SORT10:
        for a, b in layer:
            wires[a], wires[b] = jnp.minimum(wires[a], wires[b]), jnp.maximum(wires[a], wires[b])
    count = sum((w < TAB).astype(jnp.int32) for w in wires)
    most = count[:, :SHARE]
    for b in range(1, NY):
        most = jnp.maximum(most, count[:, b * SHARE : (b + 1) * SHARE])
    cnt[...] = most
    for f in range(FAN):
        packed = wires[f][:, : TGT // 2] | (wires[f][:, TGT // 2 :] << 16)
        for g in range(NZG):
            idx[g * FAN + f : g * FAN + f + 1, :] = packed[g : g + 1, :]

    for d in range(1, NY):
        at = ((y + NY - d) % NY) * 2 + c
        remote(wf.at[at], wf.at[at], s_w.at[d], r_w.at[d], partner).wait_recv()
        remote(wf.at[at], wf.at[at], s_f.at[d], r_f.at[d], partner).start()

    come(5, whole(xl, zo))
    go(15, whole(xl, zo), partner)
    come(6, whole(xr, zo))
    go(16, whole(xr, zo), partner)
    come(7, part(far, zo, 0))
    go(17, part(far, zo, 0), partner)
    come(8, part(far, zo, 1))
    go(18, part(far, zo, 1), partner)

    o = 1 - c
    owhole = lambda i, zz: tab.at[slot(i, zz), o]
    opart = lambda i, zz, h: tab.at[slot(i, zz), o, pl.ds(h * QUART, QUART)]
    come(9, owhole(x, zl))
    come(10, owhole(xl, zl))
    come(11, owhole(xr, zl))
    come(12, owhole(x, zo))
    come(13, opart(far, zl, 0))
    come(14, opart(far, zl, 1))
    come(15, owhole(xl, zo))
    come(16, owhole(xr, zo))
    come(17, opart(far, zo, 0))
    come(18, opart(far, zo, 1))
    for d in range(NY):
        at = ((y + NY - d) % NY) * 2 + 1 - c
        remote(wf.at[at], wf.at[at], s_f.at[d], r_f.at[d], partner).wait_recv()

    swap.wait_send()
    for copy in sends:
        copy.wait_send()
    for d in range(1, NZG):
        remote(nbs.at[zh], nbs.at[zh], s_n.at[d], r_n.at[d], partner).wait_send()
    for d in range(1, NY):
        remote(wf.at[k], wf.at[k], s_w.at[d], r_w.at[d], partner).wait_send()
    for d in range(NY):
        at = ((y + NY - d) % NY) * 2 + c
        remote(wf.at[at], wf.at[at], s_f.at[d], r_f.at[d], partner).wait_send()


def lookup_kernel(cnt, idx, rows, tab, psum, own, wide, acc):
    _, c, x, z = where_am_i()

    def conv(i, _):
        at = pl.multiple_of(i * 128, 128)
        wide[pl.ds(at, 128), :] = tab[pl.ds(at, 128), :].astype(jnp.float32)
        return 0

    lax.fori_loop(0, TAB // 128, conv, 0)
    wide[pl.ds(TAB, 8), :] = jnp.zeros((8, WIDE), jnp.float32)

    def eight(line, i):
        rows8 = []
        upper = []
        for b in range(NY // 2):
            v = idx[line, b * SHARE + i]
            rows8.append(wide[pl.ds(v & 0xFFFF, 1), :])
            upper.append(wide[pl.ds(v >> 16, 1), :])
        return jnp.concatenate(rows8 + upper, axis=0)

    for g in range(NZG):

        def chunk(i, _):
            total = eight(g * FAN, i) + eight(g * FAN + 1, i) + eight(g * FAN + 2, i)
            total = lax.fori_loop(3, cnt[g, i], lambda f, t: t + eight(g * FAN + f, i), total)
            acc[pl.ds(pl.multiple_of(i * NY, NY), NY), :] = total
            return 0

        lax.fori_loop(0, SHARE, chunk, 0)
        for b in range(NY):
            psum[g, b * SHARE : (b + 1) * SHARE, :] = acc[pl.ds(b, SHARE, stride=NY), :].astype(jnp.bfloat16)

    base = (x * 2 + z % 2) * ROWS

    def mine(i, _):
        got = [wide[pl.ds(base + rows[b * 128 + c * 64 + i], 1), :] for b in range(NY)]
        acc[pl.ds(pl.multiple_of(i * NY, NY), NY), :] = jnp.concatenate(got, axis=0)
        return 0

    lax.fori_loop(0, SHARE, mine, 0)
    for b in range(NY):
        own[b * SHARE : (b + 1) * SHARE, :] = acc[pl.ds(b, SHARE, stride=NY), :].astype(jnp.bfloat16)


ROOT = math.sqrt(2.0 / math.pi)


def layer_kernel(
    psum, own, wf, cot, hidden, gself, gneigh,
    rz, both, abuf, slopes, gout, gin, gsend, grecv, gred, gfull,
    s_z, r_z, s_o, r_o, s_m, r_m, s_s, r_s, s_c, r_c, s_r, r_r, s_g, r_g,
):
    y, c, x, z = where_am_i()
    zl, zh = z % 2, z // 2
    node = x * NZ + z
    partner = dev(y, 1 - c, x, z)
    at_y = lambda d: dev((y + d) % NY, c, x, z)
    feat_id = y * 2 + c
    at_node = lambda q: {"feat": feat_id, "node": q}
    barrier = pltpu.get_barrier_semaphore()
    pl.semaphore_signal(barrier, inc=1, device_id=partner, device_id_type=MESH)
    for d in range(1, NY):
        pl.semaphore_signal(barrier, inc=1, device_id=at_y(d), device_id_type=MESH)

    def greet(d, _):
        pl.semaphore_signal(barrier, inc=1, device_id=at_node((node + d) % NODES), device_id_type=MESH)
        return 0

    lax.fori_loop(1, NODES, greet, 0)
    pl.semaphore_wait(barrier, 1 + NY - 1 + NODES - 1)

    for d in range(1, NZG):
        to = dev(y, c, x, (z + 2 * d) % NZ)
        remote(psum.at[(zh + d) % NZG], rz.at[d - 1], s_z.at[d], r_z.at[d], to).start()

    def block(ref, b):
        return ref.at[pl.ds(pl.multiple_of(b * SHARE, SHARE), SHARE)]

    for d in range(1, NY):
        remote(block(own, (y + d) % NY), abuf.at[y, 0], s_o.at[d], r_o.at[d], at_y(d)).start()
    abuf[y, 0] = own[pl.ds(pl.multiple_of(y * SHARE, SHARE), SHARE), :]
    both[0] = own[...]
    for d in range(1, NZG):
        remote(psum.at[zh], rz.at[d - 1], s_z.at[d], r_z.at[d], partner).wait_recv()
    total = psum[zh].astype(jnp.float32)
    for d in range(NZG - 1):
        total = total + rz[d].astype(jnp.float32)
    both[1] = (total * (1.0 / FAN)).astype(jnp.bfloat16)
    for d in range(1, NY):
        remote(block(both.at[1], (y + d) % NY), abuf.at[y, 1], s_m.at[d], r_m.at[d], at_y(d)).start()
    abuf[y, 1] = both[1, pl.ds(pl.multiple_of(y * SHARE, SHARE), SHARE), :]
    for d in range(1, NY):
        src = (y + NY - d) % NY
        remote(abuf.at[src, 0], abuf.at[src, 0], s_o.at[d], r_o.at[d], partner).wait_recv()
        remote(abuf.at[src, 1], abuf.at[src, 1], s_m.at[d], r_m.at[d], partner).wait_recv()
    pre = jnp.zeros((SHARE, HID), jnp.float32)
    for b in range(NY):
        for s in range(2):
            w = jnp.concatenate([wf[2 * b, s], wf[2 * b + 1, s]], axis=0)
            pre = pre + jnp.dot(abuf[b, s], w, preferred_element_type=jnp.float32)
    square = pre * pre
    th = jnp.tanh(ROOT * (pre + 0.044715 * (square * pre)))
    half = 0.5 * (1.0 + th)
    hidden[...] = (pre * half).astype(jnp.bfloat16)
    dydx = half + 0.5 * pre * (1.0 - th * th) * (ROOT * (1.0 + 3.0 * 0.044715 * square))
    grads = cot[pl.ds(pl.multiple_of(feat_id * SHARE, SHARE), SHARE), :].astype(jnp.float32)
    slopes[y] = (grads * dydx).astype(jnp.bfloat16)
    for d in range(1, NY):
        remote(slopes.at[y], slopes.at[y], s_s.at[d], r_s.at[d], at_y(d)).start()
    turned = [jnp.transpose(both[s]) for s in range(2)]
    for d in range(1, NY):
        src = (y + NY - d) % NY
        remote(slopes.at[src], slopes.at[src], s_s.at[d], r_s.at[d], partner).wait_recv()
    slope = slopes[...].reshape(TGT, HID)
    keep = pl.multiple_of(c * COLS, COLS)
    give = pl.multiple_of((1 - c) * COLS, COLS)
    whole = [jnp.dot(turned[s], slope, preferred_element_type=jnp.float32) for s in range(2)]
    for s in range(2):
        gout[s] = jnp.where(c == 0, whole[s][COLS:], whole[s][:COLS]).astype(jnp.bfloat16)
    swap = remote(gout, gin, s_c, r_c, partner)
    swap.start()
    stay = [jnp.where(c == 0, whole[s][:COLS], whole[s][COLS:]) for s in range(2)]
    swap.wait_recv()
    for s in range(2):
        mine = stay[s] + gin[s].astype(jnp.float32)
        for r in range(8):
            for h in range(2):
                gsend[s * 16 + r * 2 + h] = mine[r * 8 : r * 8 + 8, h * 128 : h * 128 + 128]

    def scatter(d, _):
        to = (node + d) % NODES
        remote(gsend.at[to], grecv.at[d], s_r.at[d], r_r.at[d], at_node(to)).start()
        return 0

    lax.fori_loop(1, NODES, scatter, 0)

    def collect(d, t):
        remote(gsend.at[0], grecv.at[d], s_r.at[d], r_r.at[d], partner).wait_recv()
        return t + grecv[d]

    gfull[node] = lax.fori_loop(1, NODES, collect, gsend[node])

    def spread(d, _):
        remote(gfull.at[node], gfull.at[node], s_g.at[d], r_g.at[d], at_node((node + d) % NODES)).start()
        return 0

    lax.fori_loop(1, NODES, spread, 0)

    def arrive(d, _):
        src = (node + NODES - d) % NODES
        remote(gfull.at[src], gfull.at[src], s_g.at[d], r_g.at[d], partner).wait_recv()
        return 0

    lax.fori_loop(1, NODES, arrive, 0)
    for s, out in enumerate((gself, gneigh)):
        for r in range(8):
            for h in range(2):
                out[r * 8 : r * 8 + 8, h * 128 : h * 128 + 128] = gfull[s * 16 + r * 2 + h]

    for d in range(1, NZG):
        remote(psum.at[zh], rz.at[d - 1], s_z.at[d], r_z.at[d], partner).wait_send()
    for d in range(1, NY):
        remote(abuf.at[y, 0], abuf.at[y, 0], s_o.at[d], r_o.at[d], partner).wait_send()
        remote(abuf.at[y, 1], abuf.at[y, 1], s_m.at[d], r_m.at[d], partner).wait_send()
        remote(slopes.at[y], slopes.at[y], s_s.at[d], r_s.at[d], partner).wait_send()
    swap.wait_send()

    def drain(d, _):
        remote(gsend.at[0], grecv.at[d], s_r.at[d], r_r.at[d], partner).wait_send()
        remote(gfull.at[node], gfull.at[node], s_g.at[d], r_g.at[d], partner).wait_send()
        return 0

    lax.fori_loop(1, NODES, drain, 0)


VMEM = pl.BlockSpec(memory_space=pltpu.VMEM)
SMEM = pl.BlockSpec(memory_space=pltpu.SMEM)
DMA = pltpu.SemaphoreType.DMA


def on_device(features, self_rows, neighbours, w_self, w_neigh, cotangent):
    bf, f32, i32 = jnp.bfloat16, jnp.float32, jnp.int32
    shape = jax.ShapeDtypeStruct
    tab, idx, cnt, wf = pl.pallas_call(
        gather_kernel,
        out_shape=[
            shape((GROUP, 2, HALF, WIDE), bf),
            shape((NZG * FAN, TGT // 2), i32),
            shape((NZG, SHARE), i32),
            shape((2 * NY, 2, COLS, HID), bf),
        ],
        in_specs=[VMEM] * 4,
        out_specs=[VMEM] * 4,
        scratch_shapes=[
            pltpu.VMEM((HALF, COLS), bf),
            pltpu.VMEM((NZG, FAN, TGT), i32),
            DMA, DMA, DMA((19,)), DMA((19,)), DMA((NZG,)), DMA((NZG,)),
            DMA((NY,)), DMA((NY,)), DMA((NY,)), DMA((NY,)),
        ],
        compiler_params=pltpu.CompilerParams(collective_id=0, has_side_effects=True, vmem_limit_bytes=VM),
        name="gather_rows",
    )(features, neighbours, w_self, w_neigh)
    psum, own = pl.pallas_call(
        lookup_kernel,
        out_shape=[shape((NZG, TGT, WIDE), bf), shape((TGT, WIDE), bf)],
        in_specs=[SMEM, SMEM, SMEM, VMEM],
        out_specs=[VMEM] * 2,
        scratch_shapes=[pltpu.VMEM((TAB + 8, WIDE), f32), pltpu.VMEM((TGT, WIDE), f32)],
        compiler_params=pltpu.CompilerParams(vmem_limit_bytes=VM),
        name="lookup_rows",
    )(cnt, idx, self_rows, tab.reshape(TAB, WIDE))
    return pl.pallas_call(
        layer_kernel,
        out_shape=[shape((SHARE, HID), bf), shape((COLS, HID), f32), shape((COLS, HID), f32)],
        in_specs=[VMEM] * 4,
        out_specs=[VMEM] * 3,
        scratch_shapes=[
            pltpu.VMEM((NZG - 1, TGT, WIDE), bf),
            pltpu.VMEM((2, TGT, WIDE), bf),
            pltpu.VMEM((NY, 2, SHARE, WIDE), bf),
            pltpu.VMEM((NY, SHARE, HID), bf),
            pltpu.VMEM((2, COLS, HID), bf),
            pltpu.VMEM((2, COLS, HID), bf),
            pltpu.VMEM((NODES, 8, 128), f32),
            pltpu.VMEM((NODES, 8, 128), f32),
            pltpu.VMEM((8, 128), f32),
            pltpu.VMEM((NODES, 8, 128), f32),
            DMA((NZG,)), DMA((NZG,)),
            DMA((NY,)), DMA((NY,)), DMA((NY,)), DMA((NY,)), DMA((NY,)), DMA((NY,)),
            DMA, DMA,
            DMA((NODES,)), DMA((NODES,)), DMA((NODES,)), DMA((NODES,)),
        ],
        compiler_params=pltpu.CompilerParams(collective_id=1, has_side_effects=True, vmem_limit_bytes=VM),
        name="layer",
    )(psum, own, wf, cotangent)


def solution(mesh):
    return jax.shard_map(
        on_device,
        mesh=mesh,
        in_specs=(
            P("node", "feat"),
            P("node"),
            P(None, "node"),
            P("feat", None),
            P("feat", None),
            P("node", None),
        ),
        out_specs=(P(("node", "feat"), None), P("feat", None), P("feat", None)),
        check_vma=False,
    )
```

time: 467 us -> 127 us (0.27)
  waiting for transfers between devices: 255 us -> 0 us
  local copies, waits for them, and re-layouts: 138 us -> 6.3 us
  Pallas kernels: 0 us -> 119 us
  blocking collectives: 17.9 us -> 0 us
  starting transfers between devices: 17.9 us -> 0 us
  other arithmetic: 16.5 us -> 0 us
  between operations: 14.3 us -> 0.65 us
    psum x1 -> x0, waiting for transfers between devices: 145 us -> none  [on_device(): lax.psum(grad_self.astype(jnp.bfloat16), 'node').astype(jnp.float32)]
    pallas_call x0 -> x3, Pallas kernels: none -> 119 us  [the longest x1 55.1 us: on_device(): pl.pallas_call(layer_kernel, out_shape=[shape((SHARE, HID), bf), shape((C...]
    gather x4 -> x0, local copies, waits for them, and re-layouts: 91.9 us -> none  [the longest x2 58.7 us: on_device(): features[wanted]]
    reduce_scatter x1 -> x0, waiting for transfers between devices: 55.9 us -> none  [on_device(): lax.psum_scatter((jnp.dot(own_part, w_self, preferred_element_type=jnp.fl...]
    all_to_all x2 -> x0, waiting for transfers between devices: 53.4 us -> none  [the longest x1 44.8 us: on_device(): lax.all_to_all(features[wanted], 'node', split_axis=0, concat_axis=0, til...]
    scatter x1 -> x0, local copies, waits for them, and re-layouts: 38 us -> none  [on_device(): jnp.zeros((parts * capacity,), jnp.int32).at[place].set(local)]
    all_gather x1 -> x0, blocking collectives: 17.9 us -> none  [on_device(): piece = lax.all_gather(slope, 'feat', axis=0, tiled=True)]
    all_to_all x2 -> x0, starting transfers between devices: 17.9 us -> none  [the longest x1 13.7 us: on_device(): lax.all_to_all(requests, 'node', split_axis=0, concat_axis=0, tiled=True)]
  transfers between devices with their start and end apart: 4 -> 0, of which waited for: 4 -> 0; matrix products, arithmetic and copies ran while one was open for 1% -> 0% of each run, Pallas kernels for 0% -> 0%
where the time goes in v1:
time: 127 us; the launch traced here: 126 us
  Pallas kernels  119 us (94%)
  local copies, waits for them, and re-layouts  6.3 us (5%)
    pallas_call x1, Pallas kernels, on_device(): pl.pallas_call(layer_kernel, out_shape=[shape((SHARE, HID), bf), shape((C...  55.1 us
    pallas_call x1, Pallas kernels, on_device(): pl.pallas_call(gather_kernel, out_shape=[shape((GROUP, 2, HALF, WIDE), bf...  39.8 us
    pallas_call x1, Pallas kernels, on_device(): pl.pallas_call(lookup_kernel, out_shape=[shape((NZG, TGT, WIDE), bf), sha...  24.3 us
    unnamed x4, local copies, waits for them, and re-layouts  6.3 us

profile of v1, /device:TPU:1, one launch (start us, length us, event | category | flops | bytes accessed | tf_op | source)
XLA Modules:
  0.0 126.2 jit_solution(29050153828729040)
XLA Ops:
  0.6 2.0 %copy.9.feat = bf16[2048,64]{1,0:T(8,128)(2,1)} copy(bf16[2048,64]{0,1:T(8,128)(2,1)} %param.6) | data formatting | bytes 524288 | tf_op args[0]
  2.6 39.8 %gather_rows.1 = (bf16[8,2,1024,128]{3,2,1,0:T(8,128)(2,1)}, s32[40,256]{1,0:T(8,128)}, s32[4,64]{1,0:T(4,128)}, bf16[16,2,64,256]{3,2,1,0:T(8,128)(2,1)}) custom-call(bf16[2048,64]{1,0:T(8,128)(2,1)} %copy.9.feat, s32[10,1024]{1,0:T(8,128)} %nb.1, bf16[64,256]{1,0:T(8,128)(2,1)} %ws.1, bf16[64,256]{1,0:T(8,128)(2,1)} %wn.1), custom_call_target="tpu_custom_call" | custom-call | tf_op jit(solution)/shard_map/gather_rows/pallas_call | solution.py:389
  42.4 24.3 %lookup_rows.1 = (bf16[4,512,128]{2,1,0:T(8,128)(2,1)}, bf16[512,128]{1,0:T(8,128)(2,1)}) custom-call(s32[4,64]{1,0:T(4,128)} %get-tuple-element.9.cnt, s32[40,256]{1,0:T(8,128)} %get-tuple-element.10.idx, s32[1024]{0:T(1024)} %rows.1, bf16[16384,128]{1,0:T(8,128)(2,1)} %bitcast.1), custom_call_target="tpu_custom_call" | custom-call | tf_op jit(solution)/shard_map/lookup_rows/pallas_call | solution.py:408
  66.7 55.1 %layer.1 = (bf16[64,256]{1,0:T(8,128)(2,1)}, f32[64,256]{1,0:T(8,128)}, f32[64,256]{1,0:T(8,128)}) custom-call(bf16[4,512,128]{2,1,0:T(8,128)(2,1)} %get-tuple-element.12.psum, bf16[512,128]{1,0:T(8,128)(2,1)} %get-tuple-element.13.own, bf16[16,2,64,256]{3,2,1,0:T(8,128)(2,1)} %get-tuple-element.14.wf, bf16[1024,256]{1,0:T(8,128)(2,1)} %cot.1), custom_call_target="tpu_custom_call" | custom-call | tf_op jit(solution)/shard_map/layer/pallas_call | solution.py:417
  121.9 1.4 %copy.13 = bf16[64,256]{1,0:T(8,128)(2,1)} copy(bf16[64,256]{1,0:T(8,128)(2,1)} %get-tuple-element.18) | data formatting | bytes 65536
  123.2 1.5 %copy.14 = f32[64,256]{1,0:T(8,128)} copy(f32[64,256]{1,0:T(8,128)} %get-tuple-element.19) | data formatting | bytes 131072
  124.7 1.5 %copy.15 = f32[64,256]{1,0:T(8,128)} copy(f32[64,256]{1,0:T(8,128)} %get-tuple-element.20) | data formatting | bytes 131072

commit v2 on v0

v2 whole, which is shorter than its diff:
```python
import math

import jax
import jax.numpy as jnp
from jax import lax
from jax.experimental import pallas as pl
from jax.experimental.pallas import tpu as pltpu
from jax.sharding import PartitionSpec as P

NX, NZ, NY = 4, 8, 8
FAN = 10
PAIR = FAN // 2
ROWS = 2048
HALF = ROWS // 2
UNIT = HALF // 2
COLS = 64
WIDE = 2 * COLS
HID = 256
SHARE = 64
TGT = NY * SHARE
GROUP = 2 * NX
NZG = NZ // 2
TAB = GROUP * ROWS
QROW = COLS // NX
NS = 1
RB = SHARE // NS
MESH = pl.DeviceIdType.MESH
ROOT = math.sqrt(2.0 / math.pi)
BF, F32, I32 = jnp.bfloat16, jnp.float32, jnp.int32


def kernel(
    feat, nb, rows, ws, wn, cot, hidden, gself, gneigh,
    pieces, tab, wide, nbs, lists, idx, wf, own, theirs, stage, pin, mine, slopes, means,
    gsend, gx, gz, gq,
    s_x, r_x, s_t, r_t, s_n, r_n, s_w, r_w, s_f, r_f, s_o, r_o, s_p, r_p, s_s, r_s, s_m, r_m,
    s_gx, r_gx, s_gz, r_gz, s_gq, r_gq, s_idx,
):
    f_id, n_id = lax.axis_index("feat"), lax.axis_index("node")
    y, c, x, z = f_id // 2, f_id % 2, n_id // NZ, n_id % NZ
    zl, zh = z % 2, z // 2

    def dev(dy, dc, dx, dz):
        core = 1 - c if dc else c
        return {"feat": ((y + dy) % NY) * 2 + core, "node": ((x + dx) % NX) * NZ + (z + dz) % NZ}

    partner = dev(0, 1, 0, 0)
    right, left = dev(0, 0, 1, 0), dev(0, 0, NX - 1, 0)
    over = {"feat": f_id, "node": x * NZ + z + 1 - 2 * zl}

    def remote(src, dst, send, recv, to):
        return pltpu.make_async_remote_copy(
            src_ref=src, dst_ref=dst, send_sem=send, recv_sem=recv, device_id=to, device_id_type=MESH
        )

    def arrived(ref, recv):
        remote(ref, ref, recv, recv, partner).wait_recv()

    def left_here(ref, send):
        remote(ref, ref, send, send, partner).wait_send()

    barrier = pltpu.get_barrier_semaphore()
    friends = [partner]
    friends += [dev(0, 0, 0, d) for d in range(1, NZ)]
    friends += [dev(0, dc, d, 0) for d in range(1, NX) for dc in range(2)]
    friends += [dev(e, 0, 0, 2 * d) for d in range(NZG) for e in range(1, NY)]
    for to in friends:
        pl.semaphore_signal(barrier, inc=1, device_id=to, device_id_type=MESH)

    wf[f_id, 0] = ws[...]
    wf[f_id, 1] = wn[...]
    cuts = []
    for b in range(NY):
        lo = nb[:, b * 128 : b * 128 + 64]
        hi = nb[:, b * 128 + 64 : b * 128 + 128]
        cuts.append(jnp.where(c == 0, lo, hi))
    nbs[zh] = jnp.concatenate(cuts, axis=1)
    give = pl.multiple_of((1 - c) * HALF, HALF)
    keep = pl.multiple_of(c * HALF, HALF)
    pieces[c] = feat[:, pl.ds(keep, HALF)]

    pl.semaphore_wait(barrier, len(friends))

    swap = remote(feat.at[:, pl.ds(give, HALF)], pieces.at[c], s_x, r_x, partner)
    swap.start()
    for d in range(1, NZG):
        remote(nbs.at[zh], nbs.at[zh], s_n.at[d], r_n.at[d], dev(0, 0, 0, 2 * d)).start()
    arrived(pieces.at[1 - c], r_x)
    home = x * 2 + zl

    def turn(i, _):
        at = pl.multiple_of(i * 256, 256)
        block = pieces[:, :, pl.ds(at, 256)].reshape(WIDE, 256)
        tab[home, c, pl.ds(at, 256), :] = jnp.transpose(block)
        return 0

    lax.fori_loop(0, HALF // 256, turn, 0)

    xr, xl, far, zo = (x + 1) % NX, (x + NX - 1) % NX, (x + 2) % NX, 1 - zl

    def unit(i, zz, h, core):
        return tab.at[i * 2 + zz, core, pl.ds(h * UNIT, UNIT)]

    def widen(i, zz, h, core):
        base = ((i * 2 + zz) * 2 + core) * HALF + h * UNIT

        def step(k, _):
            at = pl.multiple_of(k * 128, 128)
            piece = tab[i * 2 + zz, core, pl.ds(h * UNIT + at, 128), :]
            wide[pl.ds(pl.multiple_of(base + at, 128), 128), :] = piece.astype(F32)
            return 0

        lax.fori_loop(0, UNIT // 128, step, 0)

    sent = []

    def go(m, i, zz, h, to):
        ref = unit(i, zz, h, c)
        remote(ref, ref, s_t.at[m], r_t.at[m], to).start()
        sent.append((ref, s_t.at[m]))

    passed = []

    def pass_on(i, zz, h):
        m = 14 + len(passed)
        go(m, i, zz, h, partner)
        passed.append((m, i, zz, h))

    def come(m, i, zz, h):
        arrived(unit(i, zz, h, c), r_t.at[m])

    go(0, x, zl, 0, right)
    go(3, x, zl, 1, left)
    go(4, x, zl, 0, over)
    go(1, x, zl, 1, right)
    go(2, x, zl, 0, left)
    go(5, x, zl, 1, over)
    pass_on(x, zl, 0)
    pass_on(x, zl, 1)
    for d in range(1, NY):
        remote(wf.at[f_id], wf.at[f_id], s_w.at[d], r_w.at[d], dev(d, 0, 0, 0)).start()
    remote(wf.at[f_id], wf.at[f_id], s_f.at[0], r_f.at[0], partner).start()
    widen(x, zl, 0, c)
    widen(x, zl, 1, c)

    for d in range(1, NZG):
        at = (zh + NZG - d) % NZG
        arrived(nbs.at[at], r_n.at[d])
    for g in range(NZG):
        n = nbs[g]
        part_of = n >> 11
        inside = ((part_of & 7) >> 1) == zh
        row = ((((part_of >> 3) << 1) | (part_of & 1)) << 11) | (n & (ROWS - 1))
        row = jnp.where(inside, row, TAB)
        lists[g * 8 : g * 8 + PAIR, :] = row[:PAIR] | (row[PAIR:] << 16)
    to_scalar = pltpu.make_async_copy(lists, idx, s_idx)
    to_scalar.start()

    arrived(unit(x, zl, 0, 1 - c), r_t.at[14])
    widen(x, zl, 0, 1 - c)
    arrived(unit(x, zl, 1, 1 - c), r_t.at[15])
    widen(x, zl, 1, 1 - c)

    def fetch_own(k, _):
        got = [
            wide[pl.ds(home * ROWS + rows[(k // 8) * 128 + c * SHARE + (k % 8) * 8 + u], 1), :] for u in range(8)
        ]
        own[pl.ds(pl.multiple_of(k * 8, 8), 8), :] = jnp.concatenate(got, axis=0)
        return 0

    come(0, xl, zl, 0)
    go(6, xl, zl, 0, right)
    pass_on(xl, zl, 0)
    come(3, xr, zl, 1)
    go(7, xr, zl, 1, left)
    pass_on(xr, zl, 1)
    come(4, x, zo, 0)
    go(8, x, zo, 0, right)
    go(9, x, zo, 0, left)
    pass_on(x, zo, 0)
    widen(xl, zl, 0, c)
    widen(xr, zl, 1, c)
    come(1, xl, zl, 1)
    pass_on(xl, zl, 1)
    come(2, xr, zl, 0)
    pass_on(xr, zl, 0)
    come(5, x, zo, 1)
    go(10, x, zo, 1, right)
    go(11, x, zo, 1, left)
    pass_on(x, zo, 1)
    lax.fori_loop(0, TGT // 8, fetch_own, 0)
    means[NS] = own[...].astype(BF).reshape(NY, SHARE, WIDE)
    theirs[y] = means[NS, y]
    for e in range(1, NY):
        remote(means.at[NS, (y + e) % NY], theirs.at[y], s_o.at[e], r_o.at[e], dev(e, 0, 0, 0)).start()
    widen(x, zo, 0, c)
    widen(xl, zl, 1, c)
    widen(xr, zl, 0, c)
    widen(x, zo, 1, c)
    come(6, far, zl, 0)
    go(12, far, zl, 0, over)
    pass_on(far, zl, 0)
    come(7, far, zl, 1)
    go(13, far, zl, 1, over)
    pass_on(far, zl, 1)
    for d in range(1, NY):
        at = ((y + NY - d) % NY) * 2 + c
        arrived(wf.at[at], r_w.at[d])
        remote(wf.at[at], wf.at[at], s_f.at[d], r_f.at[d], partner).start()
    widen(far, zl, 0, c)
    widen(far, zl, 1, c)
    come(8, xl, zo, 0)
    pass_on(xl, zo, 0)
    come(9, xr, zo, 0)
    pass_on(xr, zo, 0)
    widen(xl, zo, 0, c)
    widen(xr, zo, 0, c)
    come(10, xl, zo, 1)
    pass_on(xl, zo, 1)
    come(11, xr, zo, 1)
    pass_on(xr, zo, 1)
    come(12, far, zo, 0)
    pass_on(far, zo, 0)
    come(13, far, zo, 1)
    pass_on(far, zo, 1)
    widen(xl, zo, 1, c)
    widen(xr, zo, 1, c)
    widen(far, zo, 0, c)
    widen(far, zo, 1, c)
    for m, i, zz, h in passed[2:]:
        arrived(unit(i, zz, h, 1 - c), r_t.at[m])
        widen(i, zz, h, 1 - c)
    wide[pl.ds(TAB, 8), :] = jnp.zeros((8, WIDE), F32)
    to_scalar.wait()

    def block(g, b, s, put):
        def eight(k, _):
            out = []
            for u in range(8):
                t = b * SHARE + s * RB + k * 8 + u
                v = idx[g * 8, t]
                total = wide[pl.ds(v & 0xFFFF, 1), :] + wide[pl.ds(v >> 16, 1), :]
                for j in range(1, PAIR):
                    v = idx[g * 8 + j, t]
                    total = total + wide[pl.ds(v & 0xFFFF, 1), :]
                    total = total + wide[pl.ds(v >> 16, 1), :]
                out.append(total)
            own[pl.ds(pl.multiple_of(k * 8, 8), 8), :] = jnp.concatenate(out, axis=0)
            return 0

        lax.fori_loop(0, RB // 8, eight, 0)
        put[...] = own[pl.ds(0, RB), :].astype(BF)

    def plane(s, d):
        g = (zh + d) % NZG

        def one(e, _):
            at = (s * NZG + d) * NY + e
            block(g, (y + e) % NY, s, stage.at[at])
            remote(stage.at[at], pin.at[at], s_p.at[at], r_p.at[at], dev(e, 0, 0, 2 * d)).start()
            return 0

        lax.fori_loop(1 if d == 0 else 0, NY, one, 0)
        if d == 0:
            block(g, y, s, pin.at[s * NZG * NY])

    def activate(s):
        pre = jnp.zeros((RB, HID), F32)
        for e in range(NY):
            src = (y + NY - e) % NY
            total = jnp.zeros((RB, WIDE), F32)
            for d in range(NZG):
                at = (s * NZG + d) * NY + e
                if d or e:
                    arrived(pin.at[at], r_p.at[at])
                total = total + pin[at].astype(F32)
            mean = (total * (1.0 / FAN)).astype(BF)
            if e:
                mine[s * NY + e] = mean
                to = dev(NY - e, 0, 0, 0)
                remote(mine.at[s * NY + e], means.at[s, y], s_m.at[s * NY + e], r_m.at[s * NY + e], to).start()
            else:
                means[s, y] = mean
            w_own = jnp.concatenate([wf[2 * src, 0], wf[2 * src + 1, 0]], axis=0)
            w_mean = jnp.concatenate([wf[2 * src, 1], wf[2 * src + 1, 1]], axis=0)
            rows_own = theirs[src, s * RB : (s + 1) * RB, :]
            pre = pre + jnp.dot(rows_own, w_own, preferred_element_type=F32)
            pre = pre + jnp.dot(mean, w_mean, preferred_element_type=F32)
        square = pre * pre
        th = jnp.tanh(ROOT * (pre + 0.044715 * (square * pre)))
        half = 0.5 * (1.0 + th)
        dydx = half + 0.5 * pre * (1.0 - th * th) * (ROOT * (1.0 + 3.0 * 0.044715 * square))
        first = pl.multiple_of(f_id * SHARE + s * RB, RB)
        slopes[s, y] = (cot[pl.ds(first, RB), :].astype(F32) * dydx).astype(BF)
        for e in range(1, NY):
            at = s * NY + e
            remote(slopes.at[s, y], slopes.at[s, y], s_s.at[at], r_s.at[at], dev(e, 0, 0, 0)).start()
        hidden[s * RB : (s + 1) * RB, :] = (pre * half).astype(BF)

    def grads(s):
        turned = jnp.transpose(means[NS, :, s * RB : (s + 1) * RB, :].reshape(NY * RB, WIDE))
        for e in range(1, NY):
            src = (y + NY - e) % NY
            arrived(slopes.at[s, src], r_s.at[s * NY + e])
        slope = slopes[s].reshape(NY * RB, HID)
        g_self = jnp.dot(turned, slope, preferred_element_type=F32)
        for e in range(1, NY):
            arrived(means.at[s, (y + e) % NY], r_m.at[s * NY + e])
        turned = jnp.transpose(means[s].reshape(NY * RB, WIDE))
        return g_self, jnp.dot(turned, slope, preferred_element_type=F32)

    for d in (1, 2, 3, 0):
        plane(0, d)
    for d in range(1, NY):
        at = ((y + NY - d) % NY) * 2 + 1 - c
        arrived(wf.at[at], r_f.at[d])
    arrived(wf.at[y * 2 + 1 - c], r_f.at[0])
    for e in range(1, NY):
        arrived(theirs.at[(y + NY - e) % NY], r_o.at[e])
    activate(0)
    both = grads(0)

    for p in range(2):
        for q in range(NX):
            for w in range(2):
                at = p * COLS + q * QROW
                gsend[p * NX + q, w] = both[w][at : at + QROW].astype(BF)
    hops = [(dc, dx) for dx in range(NX) for dc in range(2) if dc or dx]
    for n, (dc, dx) in enumerate(hops):
        core = 1 - c if dc else c
        remote(gsend.at[core * NX + (x + dx) % NX], gx.at[n], s_gx.at[n], r_gx.at[n], dev(0, dc, dx, 0)).start()
    total = gsend[c * NX + x].astype(F32)
    for n in range(len(hops)):
        arrived(gx.at[n], r_gx.at[n])
        total = total + gx[n].astype(F32)
    gz[z] = total.astype(BF)
    for d in range(1, NZ):
        remote(gz.at[z], gz.at[z], s_gz.at[d], r_gz.at[d], dev(0, 0, 0, d)).start()
    for d in range(1, NZ):
        arrived(gz.at[(z + NZ - d) % NZ], r_gz.at[d])
    total = gz[0].astype(F32)
    for d in range(1, NZ):
        total = total + gz[d].astype(F32)
    gq[x] = total
    for d in range(1, NX):
        remote(gq.at[x], gq.at[x], s_gq.at[d], r_gq.at[d], dev(0, 0, d, 0)).start()
    for d in range(1, NX):
        arrived(gq.at[(x + NX - d) % NX], r_gq.at[d])
    for q in range(NX):
        gself[q * QROW : (q + 1) * QROW, :] = gq[q, 0]
        gneigh[q * QROW : (q + 1) * QROW, :] = gq[q, 1]

    left_here(feat.at[:, pl.ds(give, HALF)], s_x)
    for ref, sem in sent:
        left_here(ref, sem)
    for d in range(1, NZG):
        left_here(nbs.at[zh], s_n.at[d])
    for d in range(1, NY):
        left_here(wf.at[f_id], s_w.at[d])
        left_here(theirs.at[y], s_o.at[d])
    for d in range(NY):
        left_here(wf.at[f_id], s_f.at[d])

    def drain(at, _):
        left_here(stage.at[at], s_p.at[at])
        return 0

    for s in range(NS):
        lax.fori_loop(s * NZG * NY + 1, (s + 1) * NZG * NY, drain, 0)
        for e in range(1, NY):
            left_here(slopes.at[s, y], s_s.at[s * NY + e])
            left_here(mine.at[s * NY + e], s_m.at[s * NY + e])
    for n in range(len(hops)):
        left_here(gsend.at[0], s_gx.at[n])
    for d in range(1, NZ):
        left_here(gz.at[z], s_gz.at[d])
    for d in range(1, NX):
        left_here(gq.at[x], s_gq.at[d])


def hand_over(a, b, c, out_a, out_b, out_c):
    out_a[...] = a[...]
    out_b[...] = b[...]
    out_c[...] = c[...]


VMEM = pl.BlockSpec(memory_space=pltpu.VMEM)
SMEM = pl.BlockSpec(memory_space=pltpu.SMEM)


def sems(*counts):
    return [pltpu.SemaphoreType.DMA((n,)) if n else pltpu.SemaphoreType.DMA for n in counts for _ in range(2)]


def on_device(features, self_rows, neighbours, w_self, w_neigh, cotangent):
    shape = jax.ShapeDtypeStruct
    outs = [shape((SHARE, HID), BF), shape((COLS, HID), F32), shape((COLS, HID), F32)]
    got = pl.pallas_call(
        kernel,
        out_shape=outs,
        in_specs=[VMEM, VMEM, SMEM, VMEM, VMEM, VMEM],
        out_specs=[VMEM] * 3,
        scratch_shapes=[
            pltpu.VMEM((2, COLS, HALF), BF),
            pltpu.VMEM((GROUP, 2, HALF, WIDE), BF),
            pltpu.VMEM((TAB + 8, WIDE), F32),
            pltpu.VMEM((NZG, FAN, TGT), I32),
            pltpu.VMEM((NZG * 8, TGT), I32),
            pltpu.SMEM((NZG * 8, TGT), I32),
            pltpu.VMEM((2 * NY, 2, COLS, HID), BF),
            pltpu.VMEM((TGT, WIDE), F32),
            pltpu.VMEM((NY, SHARE, WIDE), BF),
            pltpu.VMEM((NS * NZG * NY, RB, WIDE), BF),
            pltpu.VMEM((NS * NZG * NY, RB, WIDE), BF),
            pltpu.VMEM((NS * NY, RB, WIDE), BF),
            pltpu.VMEM((NS, NY, RB, HID), BF),
            pltpu.VMEM((NS + 1, NY, SHARE, WIDE), BF),
            pltpu.VMEM((2 * NX, 2, QROW, HID), BF),
            pltpu.VMEM((2 * NX - 1, 2, QROW, HID), BF),
            pltpu.VMEM((NZ, 2, QROW, HID), BF),
            pltpu.VMEM((NX, 2, QROW, HID), F32),
            *sems(0, 30, NZG, NY, NY, NY, NS * NZG * NY, NS * NY, NS * NY, 2 * NX - 1, NZ, NX),
            pltpu.SemaphoreType.DMA,
        ],
        compiler_params=pltpu.CompilerParams(collective_id=0, has_side_effects=True, vmem_limit_bytes=56 * 2**20),
        name="layer",
    )(features.T, neighbours, self_rows, w_self, w_neigh, cotangent)
    return tuple(
        pl.pallas_call(hand_over, out_shape=outs, in_specs=[VMEM] * 3, out_specs=[VMEM] * 3, name="results")(*got)
    )


def solution(mesh):
    return jax.shard_map(
        on_device,
        mesh=mesh,
        in_specs=(
            P("node", "feat"),
            P("node"),
            P(None, "node"),
            P("feat", None),
            P("feat", None),
            P("node", None),
        ),
        out_specs=(P(("node", "feat"), None), P("feat", None), P("feat", None)),
        check_vma=False,
    )
```

time: 467 us -> 111 us (0.24)
  waiting for transfers between devices: 255 us -> 0 us
  local copies, waits for them, and re-layouts: 138 us -> 0 us
  Pallas kernels: 0 us -> 110 us
  blocking collectives: 17.9 us -> 0 us
  starting transfers between devices: 17.9 us -> 0 us
  other arithmetic: 16.5 us -> 0 us
  between operations: 14.3 us -> 0.64 us
    psum x1 -> x0, waiting for transfers between devices: 145 us -> none  [on_device(): lax.psum(grad_self.astype(jnp.bfloat16), 'node').astype(jnp.float32)]
    pallas_call x0 -> x2, Pallas kernels: none -> 110 us  [the longest x1 108 us: on_device(): pl.pallas_call(kernel, out_shape=outs, in_specs=[VMEM, VMEM, SMEM, VMEM,...]
    gather x4 -> x0, local copies, waits for them, and re-layouts: 91.9 us -> none  [the longest x2 58.7 us: on_device(): features[wanted]]
    reduce_scatter x1 -> x0, waiting for transfers between devices: 55.9 us -> none  [on_device(): lax.psum_scatter((jnp.dot(own_part, w_self, preferred_element_type=jnp.fl...]
    all_to_all x2 -> x0, waiting for transfers between devices: 53.4 us -> none  [the longest x1 44.8 us: on_device(): lax.all_to_all(features[wanted], 'node', split_axis=0, concat_axis=0, til...]
    scatter x1 -> x0, local copies, waits for them, and re-layouts: 38 us -> none  [on_device(): jnp.zeros((parts * capacity,), jnp.int32).at[place].set(local)]
    all_gather x1 -> x0, blocking collectives: 17.9 us -> none  [on_device(): piece = lax.all_gather(slope, 'feat', axis=0, tiled=True)]
    all_to_all x2 -> x0, starting transfers between devices: 17.9 us -> none  [the longest x1 13.7 us: on_device(): lax.all_to_all(requests, 'node', split_axis=0, concat_axis=0, tiled=True)]
  transfers between devices with their start and end apart: 4 -> 0, of which waited for: 4 -> 0; matrix products, arithmetic and copies ran while one was open for 1% -> 0% of each run, Pallas kernels for 0% -> 0%
where the time goes in v2:
time: 111 us; the launch traced here: 110 us
  Pallas kernels  110 us (99%)
    pallas_call x1, Pallas kernels, on_device(): pl.pallas_call(kernel, out_shape=outs, in_specs=[VMEM, VMEM, SMEM, VMEM,...  108 us

profile of v2, /device:TPU:1, one launch (start us, length us, event | category | flops | bytes accessed | tf_op | source)
XLA Modules:
  0.0 110.3 jit_solution(15632424559205351721)
XLA Ops:
  0.6 108.1 %layer.1 = (bf16[64,256]{1,0:T(8,128)(2,1)}, f32[64,256]{1,0:T(8,128)}, f32[64,256]{1,0:T(8,128)}) custom-call(bf16[64,2048]{1,0:T(8,128)(2,1)} %bitcast.1, s32[10,1024]{1,0:T(8,128)} %nb.1, s32[1024]{0:T(1024)} %rows.1, bf16[64,256]{1,0:T(8,128)(2,1)} %ws.1, bf16[64,256]{1,0:T(8,128)(2,1)} %wn.1, bf16[1024,256]{1,0:T(8,128)(2,1)} %cot.1), custom_call_target="tpu_custom_call" | custom-call | tf_op jit(solution)/shard_map/layer/pallas_call | solution.py:398
  108.8 1.6 %results.1 = (bf16[64,256]{1,0:T(8,128)(2,1)}, f32[64,256]{1,0:T(8,128)}, f32[64,256]{1,0:T(8,128)}) custom-call(bf16[64,256]{1,0:T(8,128)(2,1)} %get-tuple-element.6.a, f32[64,256]{1,0:T(8,128)} %get-tuple-element.7.b, f32[64,256]{1,0:T(8,128)} %get-tuple-element.8.c), custom_call_target="tpu_custom_call" | custom-call | tf_op jit(solution)/shard_map/results/pallas_call | solution.py:429

commit v3 on v2

--- a/solution.py
+++ b/solution.py
@@ -9,7 +9,6 @@
 
 NX, NZ, NY = 4, 8, 8
 FAN = 10
-PAIR = FAN // 2
 ROWS = 2048
 HALF = ROWS // 2
 UNIT = HALF // 2
@@ -24,6 +23,8 @@
 QROW = COLS // NX
 NS = 1
 RB = SHARE // NS
+AT_ONCE = 8
+LISTS = NZG * FAN * TGT
 MESH = pl.DeviceIdType.MESH
 ROOT = math.sqrt(2.0 / math.pi)
 BF, F32, I32 = jnp.bfloat16, jnp.float32, jnp.int32
@@ -31,7 +32,7 @@
 
 def kernel(
     feat, nb, rows, ws, wn, cot, hidden, gself, gneigh,
-    pieces, tab, wide, nbs, lists, idx, wf, own, theirs, stage, pin, mine, slopes, means,
+    pieces, tab, wide, nbs, lists, idx, wf, own, theirs, stage, pin, mine, slopes, means, mates,
     gsend, gx, gz, gq,
     s_x, r_x, s_t, r_t, s_n, r_n, s_w, r_w, s_f, r_f, s_o, r_o, s_p, r_p, s_s, r_s, s_m, r_m,
     s_gx, r_gx, s_gz, r_gz, s_gq, r_gq, s_idx,
@@ -129,20 +130,38 @@
     def come(m, i, zz, h):
         arrived(unit(i, zz, h, c), r_t.at[m])
 
+    def fetch_own(k, _):
+        first = (k // 8) * 128 + c * SHARE + (k % 8) * 8
+        for u in range(8):
+            own[pl.ds(k * 8 + u, 1), :] = wide[pl.ds(home * ROWS + rows[first + u], 1), :]
+        return 0
+
     go(0, x, zl, 0, right)
     go(3, x, zl, 1, left)
     go(4, x, zl, 0, over)
-    go(1, x, zl, 1, right)
-    go(2, x, zl, 0, left)
     go(5, x, zl, 1, over)
     pass_on(x, zl, 0)
     pass_on(x, zl, 1)
-    for d in range(1, NY):
-        remote(wf.at[f_id], wf.at[f_id], s_w.at[d], r_w.at[d], dev(d, 0, 0, 0)).start()
-    remote(wf.at[f_id], wf.at[f_id], s_f.at[0], r_f.at[0], partner).start()
     widen(x, zl, 0, c)
     widen(x, zl, 1, c)
-
+    arrived(unit(x, zl, 0, 1 - c), r_t.at[14])
+    widen(x, zl, 0, 1 - c)
+    arrived(unit(x, zl, 1, 1 - c), r_t.at[15])
+    widen(x, zl, 1, 1 - c)
+    go(1, x, zl, 1, right)
+    go(2, x, zl, 0, left)
+
+    lax.fori_loop(0, TGT // 8, fetch_own, 0)
+    mates[...] = own[...].astype(BF).reshape(NY, SHARE, WIDE)
+    theirs[y] = mates[y]
+    for e in range(1, NY):
+        remote(mates.at[(y + e) % NY], theirs.at[y], s_o.at[e], r_o.at[e], dev(e, 0, 0, 0)).start()
+    come(0, xl, zl, 0)
+    go(6, xl, zl, 0, right)
+    come(3, xr, zl, 1)
+    go(7, xr, zl, 1, left)
+    pass_on(xl, zl, 0)
+    pass_on(xr, zl, 1)
     for d in range(1, NZG):
         at = (zh + NZG - d) % NZG
         arrived(nbs.at[at], r_n.at[d])
@@ -151,141 +170,122 @@
         part_of = n >> 11
         inside = ((part_of & 7) >> 1) == zh
         row = ((((part_of >> 3) << 1) | (part_of & 1)) << 11) | (n & (ROWS - 1))
-        row = jnp.where(inside, row, TAB)
-        lists[g * 8 : g * 8 + PAIR, :] = row[:PAIR] | (row[PAIR:] << 16)
-    to_scalar = pltpu.make_async_copy(lists, idx, s_idx)
-    to_scalar.start()
-
-    arrived(unit(x, zl, 0, 1 - c), r_t.at[14])
-    widen(x, zl, 0, 1 - c)
-    arrived(unit(x, zl, 1, 1 - c), r_t.at[15])
-    widen(x, zl, 1, 1 - c)
-
-    def fetch_own(k, _):
-        got = [
-            wide[pl.ds(home * ROWS + rows[(k // 8) * 128 + c * SHARE + (k % 8) * 8 + u], 1), :] for u in range(8)
-        ]
-        own[pl.ds(pl.multiple_of(k * 8, 8), 8), :] = jnp.concatenate(got, axis=0)
-        return 0
-
-    come(0, xl, zl, 0)
-    go(6, xl, zl, 0, right)
-    pass_on(xl, zl, 0)
-    come(3, xr, zl, 1)
-    go(7, xr, zl, 1, left)
-    pass_on(xr, zl, 1)
+        lists[g] = jnp.where(inside, row, TAB)
+    to_scalar = [
+        pltpu.make_async_copy(lists.at[g, f], idx.at[pl.ds((g * FAN + f) * TGT, TGT)], s_idx.at[g * FAN + f])
+        for g in range(NZG)
+        for f in range(FAN)
+    ]
+    for copy in to_scalar:
+        copy.start()
+
+    for d in range(1, NY):
+        remote(wf.at[f_id], wf.at[f_id], s_w.at[d], r_w.at[d], dev(d, 0, 0, 0)).start()
+    remote(wf.at[f_id], wf.at[f_id], s_f.at[0], r_f.at[0], partner).start()
     come(4, x, zo, 0)
-    go(8, x, zo, 0, right)
-    go(9, x, zo, 0, left)
     pass_on(x, zo, 0)
+    come(5, x, zo, 1)
+    pass_on(x, zo, 1)
     widen(xl, zl, 0, c)
     widen(xr, zl, 1, c)
+    widen(x, zo, 0, c)
     come(1, xl, zl, 1)
     pass_on(xl, zl, 1)
     come(2, xr, zl, 0)
     pass_on(xr, zl, 0)
-    come(5, x, zo, 1)
+    come(6, far, zl, 0)
+    go(12, far, zl, 0, over)
+    come(7, far, zl, 1)
+    go(13, far, zl, 1, over)
+    go(8, x, zo, 0, right)
+    go(11, x, zo, 1, left)
     go(10, x, zo, 1, right)
-    go(11, x, zo, 1, left)
-    pass_on(x, zo, 1)
-    lax.fori_loop(0, TGT // 8, fetch_own, 0)
-    means[NS] = own[...].astype(BF).reshape(NY, SHARE, WIDE)
-    theirs[y] = means[NS, y]
-    for e in range(1, NY):
-        remote(means.at[NS, (y + e) % NY], theirs.at[y], s_o.at[e], r_o.at[e], dev(e, 0, 0, 0)).start()
-    widen(x, zo, 0, c)
+    go(9, x, zo, 0, left)
+    pass_on(far, zl, 0)
+    pass_on(far, zl, 1)
+    widen(x, zo, 1, c)
     widen(xl, zl, 1, c)
     widen(xr, zl, 0, c)
-    widen(x, zo, 1, c)
-    come(6, far, zl, 0)
-    go(12, far, zl, 0, over)
-    pass_on(far, zl, 0)
-    come(7, far, zl, 1)
-    go(13, far, zl, 1, over)
-    pass_on(far, zl, 1)
-    for d in range(1, NY):
-        at = ((y + NY - d) % NY) * 2 + c
-        arrived(wf.at[at], r_w.at[d])
-        remote(wf.at[at], wf.at[at], s_f.at[d], r_f.at[d], partner).start()
     widen(far, zl, 0, c)
     widen(far, zl, 1, c)
-    come(8, xl, zo, 0)
-    pass_on(xl, zo, 0)
-    come(9, xr, zo, 0)
-    pass_on(xr, zo, 0)
-    widen(xl, zo, 0, c)
-    widen(xr, zo, 0, c)
-    come(10, xl, zo, 1)
-    pass_on(xl, zo, 1)
-    come(11, xr, zo, 1)
-    pass_on(xr, zo, 1)
+    order = ((8, xl, 0), (11, xr, 1), (10, xl, 1), (9, xr, 0))
+    for m, i, h in order:
+        come(m, i, zo, h)
+        pass_on(i, zo, h)
     come(12, far, zo, 0)
     pass_on(far, zo, 0)
+    for m, i, h in order:
+        widen(i, zo, h, c)
     come(13, far, zo, 1)
     pass_on(far, zo, 1)
-    widen(xl, zo, 1, c)
-    widen(xr, zo, 1, c)
     widen(far, zo, 0, c)
     widen(far, zo, 1, c)
     for m, i, zz, h in passed[2:]:
         arrived(unit(i, zz, h, 1 - c), r_t.at[m])
         widen(i, zz, h, 1 - c)
     wide[pl.ds(TAB, 8), :] = jnp.zeros((8, WIDE), F32)
-    to_scalar.wait()
-
-    def block(g, b, s, put):
-        def eight(k, _):
-            out = []
-            for u in range(8):
-                t = b * SHARE + s * RB + k * 8 + u
-                v = idx[g * 8, t]
-                total = wide[pl.ds(v & 0xFFFF, 1), :] + wide[pl.ds(v >> 16, 1), :]
-                for j in range(1, PAIR):
-                    v = idx[g * 8 + j, t]
-                    total = total + wide[pl.ds(v & 0xFFFF, 1), :]
-                    total = total + wide[pl.ds(v >> 16, 1), :]
-                out.append(total)
-            own[pl.ds(pl.multiple_of(k * 8, 8), 8), :] = jnp.concatenate(out, axis=0)
+    for copy in to_scalar:
+        copy.wait()
+
+    def total_of(g, b, s):
+        start = g * (FAN * TGT) + b * SHARE + s * RB
+
+        def some(k, _):
+            first = start + k * AT_ONCE
+            for u in range(AT_ONCE):
+                total = None
+                for f in range(FAN):
+                    skip = f * TGT + u
+                    row = wide[pl.ds(idx.at[pl.ds(skip, LISTS - skip)][first], 1), :]
+                    total = row if total is None else total + row
+                own[pl.ds(k * AT_ONCE + u, 1), :] = total
             return 0
 
-        lax.fori_loop(0, RB // 8, eight, 0)
-        put[...] = own[pl.ds(0, RB), :].astype(BF)
+        lax.fori_loop(0, RB // AT_ONCE, some, 0)
 
     def plane(s, d):
         g = (zh + d) % NZG
 
         def one(e, _):
             at = (s * NZG + d) * NY + e
-            block(g, (y + e) % NY, s, stage.at[at])
-            remote(stage.at[at], pin.at[at], s_p.at[at], r_p.at[at], dev(e, 0, 0, 2 * d)).start()
+            total_of(g, (y + e) % NY, s)
+            stage[at] = own[pl.ds(0, RB), :].astype(BF)
+            remote(stage.at[at], pin.at[at], s_p.at[at], r_p.at[at], dev(0, 0, 0, 2 * d)).start()
             return 0
 
-        lax.fori_loop(1 if d == 0 else 0, NY, one, 0)
-        if d == 0:
-            block(g, y, s, pin.at[s * NZG * NY])
+        lax.fori_loop(0, NY, one, 0)
+
+    def finish(s, e):
+        b = (y + e) % NY
+        total_of(zh, b, s)
+        total = own[pl.ds(0, RB), :]
+        for d in range(1, NZG):
+            at = (s * NZG + d) * NY + e
+            arrived(pin.at[at], r_p.at[at])
+            total = total + pin[at].astype(F32)
+        means[s, b] = (total * (1.0 / FAN)).astype(BF)
+
+    def home_plane(s):
+        def one(e, _):
+            at = s * NY + e
+            finish(s, e)
+            remote(means.at[s, (y + e) % NY], mine.at[s, y], s_m.at[at], r_m.at[at], dev(e, 0, 0, 0)).start()
+            return 0
+
+        lax.fori_loop(1, NY, one, 0)
+        finish(s, 0)
+        mine[s, y] = means[s, y]
 
     def activate(s):
         pre = jnp.zeros((RB, HID), F32)
         for e in range(NY):
             src = (y + NY - e) % NY
-            total = jnp.zeros((RB, WIDE), F32)
-            for d in range(NZG):
-                at = (s * NZG + d) * NY + e
-                if d or e:
-                    arrived(pin.at[at], r_p.at[at])
-                total = total + pin[at].astype(F32)
-            mean = (total * (1.0 / FAN)).astype(BF)
-            if e:
-                mine[s * NY + e] = mean
-                to = dev(NY - e, 0, 0, 0)
-                remote(mine.at[s * NY + e], means.at[s, y], s_m.at[s * NY + e], r_m.at[s * NY + e], to).start()
-            else:
-                means[s, y] = mean
             w_own = jnp.concatenate([wf[2 * src, 0], wf[2 * src + 1, 0]], axis=0)
             w_mean = jnp.concatenate([wf[2 * src, 1], wf[2 * src + 1, 1]], axis=0)
-            rows_own = theirs[src, s * RB : (s + 1) * RB, :]
-            pre = pre + jnp.dot(rows_own, w_own, preferred_element_type=F32)
-            pre = pre + jnp.dot(mean, w_mean, preferred_element_type=F32)
+            pre = pre + jnp.dot(theirs[src, s * RB : (s + 1) * RB, :], w_own, preferred_element_type=F32)
+            if e:
+                arrived(mine.at[s, src], r_m.at[s * NY + e])
+            pre = pre + jnp.dot(mine[s, src], w_mean, preferred_element_type=F32)
         square = pre * pre
         th = jnp.tanh(ROOT * (pre + 0.044715 * (square * pre)))
         half = 0.5 * (1.0 + th)
@@ -298,19 +298,22 @@
         hidden[s * RB : (s + 1) * RB, :] = (pre * half).astype(BF)
 
     def grads(s):
-        turned = jnp.transpose(means[NS, :, s * RB : (s + 1) * RB, :].reshape(NY * RB, WIDE))
+        mates_turned = jnp.transpose(mates[:, s * RB : (s + 1) * RB, :].reshape(NY * RB, WIDE))
+        means_turned = jnp.transpose(means[s].reshape(NY * RB, WIDE))
         for e in range(1, NY):
             src = (y + NY - e) % NY
             arrived(slopes.at[s, src], r_s.at[s * NY + e])
         slope = slopes[s].reshape(NY * RB, HID)
-        g_self = jnp.dot(turned, slope, preferred_element_type=F32)
-        for e in range(1, NY):
-            arrived(means.at[s, (y + e) % NY], r_m.at[s * NY + e])
-        turned = jnp.transpose(means[s].reshape(NY * RB, WIDE))
-        return g_self, jnp.dot(turned, slope, preferred_element_type=F32)
-
-    for d in (1, 2, 3, 0):
-        plane(0, d)
+        return [jnp.dot(t, slope, preferred_element_type=F32) for t in (mates_turned, means_turned)]
+
+    plane(0, 2)
+    plane(0, 1)
+    for d in range(1, NY):
+        at = ((y + NY - d) % NY) * 2 + c
+        arrived(wf.at[at], r_w.at[d])
+        remote(wf.at[at], wf.at[at], s_f.at[d], r_f.at[d], partner).start()
+    plane(0, 3)
+    home_plane(0)
     for d in range(1, NY):
         at = ((y + NY - d) % NY) * 2 + 1 - c
         arrived(wf.at[at], r_f.at[d])
@@ -366,10 +369,10 @@
         return 0
 
     for s in range(NS):
-        lax.fori_loop(s * NZG * NY + 1, (s + 1) * NZG * NY, drain, 0)
+        lax.fori_loop((s * NZG + 1) * NY, (s + 1) * NZG * NY, drain, 0)
         for e in range(1, NY):
             left_here(slopes.at[s, y], s_s.at[s * NY + e])
-            left_here(mine.at[s * NY + e], s_m.at[s * NY + e])
+            left_here(mine.at[s, y], s_m.at[s * NY + e])
     for n in range(len(hops)):
         left_here(gsend.at[0], s_gx.at[n])
     for d in range(1, NZ):
@@ -405,22 +408,23 @@
             pltpu.VMEM((GROUP, 2, HALF, WIDE), BF),
             pltpu.VMEM((TAB + 8, WIDE), F32),
             pltpu.VMEM((NZG, FAN, TGT), I32),
-            pltpu.VMEM((NZG * 8, TGT), I32),
-            pltpu.SMEM((NZG * 8, TGT), I32),
+            pltpu.VMEM((NZG, FAN, TGT), I32),
+            pltpu.SMEM((LISTS,), I32),
             pltpu.VMEM((2 * NY, 2, COLS, HID), BF),
             pltpu.VMEM((TGT, WIDE), F32),
             pltpu.VMEM((NY, SHARE, WIDE), BF),
             pltpu.VMEM((NS * NZG * NY, RB, WIDE), BF),
             pltpu.VMEM((NS * NZG * NY, RB, WIDE), BF),
-            pltpu.VMEM((NS * NY, RB, WIDE), BF),
+            pltpu.VMEM((NS, NY, RB, WIDE), BF),
             pltpu.VMEM((NS, NY, RB, HID), BF),
-            pltpu.VMEM((NS + 1, NY, SHARE, WIDE), BF),
+            pltpu.VMEM((NS, NY, RB, WIDE), BF),
+            pltpu.VMEM((NY, SHARE, WIDE), BF),
             pltpu.VMEM((2 * NX, 2, QROW, HID), BF),
             pltpu.VMEM((2 * NX - 1, 2, QROW, HID), BF),
             pltpu.VMEM((NZ, 2, QROW, HID), BF),
             pltpu.VMEM((NX, 2, QROW, HID), F32),
             *sems(0, 30, NZG, NY, NY, NY, NS * NZG * NY, NS * NY, NS * NY, 2 * NX - 1, NZ, NX),
-            pltpu.SemaphoreType.DMA,
+            pltpu.SemaphoreType.DMA((NZG * FAN,)),
         ],
         compiler_params=pltpu.CompilerParams(collective_id=0, has_side_effects=True, vmem_limit_bytes=56 * 2**20),
         name="layer",

time: 111 us -> 88.4 us (0.80)
  Pallas kernels: 110 us -> 87.6 us
    pallas_call x1, Pallas kernels: 108 us -> 86 us  [on_device(): pl.pallas_call(kernel, out_shape=outs, in_specs=[VMEM, VMEM, SMEM, VMEM,...]
where the time goes in v3:
time: 88.4 us; the launch traced here: 88.2 us
  Pallas kernels  87.6 us (99%)
    pallas_call x1, Pallas kernels, on_device(): pl.pallas_call(kernel, out_shape=outs, in_specs=[VMEM, VMEM, SMEM, VMEM,...  86 us

profile of v3, /device:TPU:1, one launch (start us, length us, event | category | flops | bytes accessed | tf_op | source)
XLA Modules:
  0.0 88.2 jit_solution(12710025359445916066)
XLA Ops:
  0.6 86.0 %layer.1 = (bf16[64,256]{1,0:T(8,128)(2,1)}, f32[64,256]{1,0:T(8,128)}, f32[64,256]{1,0:T(8,128)}) custom-call(bf16[64,2048]{1,0:T(8,128)(2,1)} %bitcast.1, s32[10,1024]{1,0:T(8,128)} %nb.1, s32[1024]{0:T(1024)} %rows.1, bf16[64,256]{1,0:T(8,128)(2,1)} %ws.1, bf16[64,256]{1,0:T(8,128)(2,1)} %wn.1, bf16[1024,256]{1,0:T(8,128)(2,1)} %cot.1), custom_call_target="tpu_custom_call" | custom-call | tf_op jit(solution)/shard_map/layer/pallas_call | solution.py:401
  86.6 1.6 %results.1 = (bf16[64,256]{1,0:T(8,128)(2,1)}, f32[64,256]{1,0:T(8,128)}, f32[64,256]{1,0:T(8,128)}) custom-call(bf16[64,256]{1,0:T(8,128)(2,1)} %get-tuple-element.6.a, f32[64,256]{1,0:T(8,128)} %get-tuple-element.7.b, f32[64,256]{1,0:T(8,128)} %get-tuple-element.8.c), custom_call_target="tpu_custom_call" | custom-call | tf_op jit(solution)/shard_map/results/pallas_call | solution.py:433

commit v4 on v3

v4 whole, which is shorter than its diff:
```python
import math

import jax
import jax.numpy as jnp
from jax import lax
from jax.experimental import pallas as pl
from jax.experimental.pallas import tpu as pltpu
from jax.sharding import PartitionSpec as P

NX, NZ, NY = 4, 8, 8
FAN = 10
PAIR = FAN // 2
ROWS = 2048
HALF = ROWS // 2
UNIT = HALF // 2
COLS = 64
WIDE = 2 * COLS
HID = 256
SHARE = 64
TGT = NY * SHARE
GROUP = 2 * NX
NZG = NZ // 2
TAB = GROUP * ROWS
QROW = COLS // NX
NS = 1
RB = SHARE // NS
AT_ONCE = 8
LISTS = NZG * FAN * TGT
MESH = pl.DeviceIdType.MESH
ROOT = math.sqrt(2.0 / math.pi)
BF, F32, I32 = jnp.bfloat16, jnp.float32, jnp.int32


def kernel(
    feat, nb, rows, ws, wn, cot, hidden, gself, gneigh,
    all_nb, my_cot, pieces, tab, wide, nbs, lists, idx, wf, own, theirs, stage, pin, mine, slopes, means, mates,
    gsend, gx, gz, gq,
    s_x, r_x, s_t, r_t, s_h, r_h, s_n, r_n, s_w, r_w, s_f, r_f, s_o, r_o, s_p, r_p, s_s, r_s, s_m, r_m,
    s_gx, r_gx, s_gz, r_gz, s_gq, r_gq, s_idx, s_in,
):
    f_id, n_id = lax.axis_index("feat"), lax.axis_index("node")
    y, c, x, z = f_id // 2, f_id % 2, n_id // NZ, n_id % NZ
    zl, zh = z % 2, z // 2

    def dev(dy, dc, dx, dz):
        core = 1 - c if dc else c
        return {"feat": ((y + dy) % NY) * 2 + core, "node": ((x + dx) % NX) * NZ + (z + dz) % NZ}

    partner = dev(0, 1, 0, 0)
    right, left = dev(0, 0, 1, 0), dev(0, 0, NX - 1, 0)
    over = {"feat": f_id, "node": x * NZ + z + 1 - 2 * zl}

    def remote(src, dst, send, recv, to):
        return pltpu.make_async_remote_copy(
            src_ref=src, dst_ref=dst, send_sem=send, recv_sem=recv, device_id=to, device_id_type=MESH
        )

    def arrived(ref, recv):
        remote(ref, ref, recv, recv, partner).wait_recv()

    def left_here(ref, send):
        remote(ref, ref, send, send, partner).wait_send()

    barrier = pltpu.get_barrier_semaphore()
    friends = [partner]
    friends += [dev(0, 0, 0, d) for d in range(1, NZ)]
    friends += [dev(0, dc, d, 0) for d in range(1, NX) for dc in range(2)]
    friends += [dev(e, 0, 0, 2 * d) for d in range(NZG) for e in range(1, NY)]
    for to in friends:
        pl.semaphore_signal(barrier, inc=1, device_id=to, device_id_type=MESH)

    give = pl.multiple_of((1 - c) * HALF, HALF)
    keep = pl.multiple_of(c * HALF, HALF)
    loads = [
        pltpu.make_async_copy(src, dst, s_in.at[n])
        for n, (src, dst) in enumerate(
            (
                (feat.at[:, pl.ds(keep, HALF)], pieces.at[c]),
                (nb, all_nb),
                (ws, wf.at[f_id, 0]),
                (wn, wf.at[f_id, 1]),
                (cot.at[pl.ds(pl.multiple_of(f_id * SHARE, SHARE), SHARE)], my_cot),
            )
        )
    ]
    for load in loads:
        load.start()

    pl.semaphore_wait(barrier, len(friends))

    swap = remote(feat.at[:, pl.ds(give, HALF)], pieces.at[c], s_x, r_x, partner)
    swap.start()
    loads[0].wait()
    arrived(pieces.at[1 - c], r_x)
    home = x * 2 + zl

    def turn(i, _):
        at = pl.multiple_of(i * 256, 256)
        block = pieces[:, :, pl.ds(at, 256)].reshape(WIDE, 256)
        tab[home, c, pl.ds(at, 256), :] = jnp.transpose(block)
        return 0

    lax.fori_loop(0, HALF // 256, turn, 0)

    xr, xl, far, zo = (x + 1) % NX, (x + NX - 1) % NX, (x + 2) % NX, 1 - zl

    def unit(i, zz, h, core):
        return tab.at[i * 2 + zz, core, pl.ds(h * UNIT, UNIT)]

    def widen(i, zz, h, core):
        base = ((i * 2 + zz) * 2 + core) * HALF + h * UNIT

        def step(k, _):
            at = pl.multiple_of(k * 128, 128)
            piece = tab[i * 2 + zz, core, pl.ds(h * UNIT + at, 128), :]
            wide[pl.ds(pl.multiple_of(base + at, 128), 128), :] = piece.astype(F32)
            return 0

        lax.fori_loop(0, UNIT // 128, step, 0)

    def go(m, i, zz, h, to):
        ref = unit(i, zz, h, c)
        remote(ref, ref, s_t.at[m // 2], r_t.at[m], to).start()

    def passing(i, zz):
        return s_h.at[i * 2 + zz], r_h.at[i * 2 + zz]

    def pass_on(i, zz, h):
        ref = unit(i, zz, h, c)
        send, recv = passing(i, zz)
        remote(ref, ref, send, recv, partner).start()

    def taken(i, zz):
        arrived(tab.at[i * 2 + zz, 1 - c], passing(i, zz)[1])
        for h in range(2):
            widen(i, zz, h, 1 - c)

    def come(m, i, zz, h):
        arrived(unit(i, zz, h, c), r_t.at[m])

    def fetch_own(k, _):
        first = (k // 8) * 128 + c * SHARE + (k % 8) * 8
        for u in range(8):
            own[pl.ds(k * 8 + u, 1), :] = wide[pl.ds(home * ROWS + rows[first + u], 1), :]
        return 0

    go(0, x, zl, 0, right)
    go(3, x, zl, 1, left)
    go(4, x, zl, 0, over)
    pass_on(x, zl, 0)
    pass_on(x, zl, 1)

    loads[1].wait()
    cuts = []
    for b in range(NY):
        lo = all_nb[:, b * 128 : b * 128 + 64]
        hi = all_nb[:, b * 128 + 64 : b * 128 + 128]
        cuts.append(jnp.where(c == 0, lo, hi))
    named = jnp.concatenate(cuts, axis=1)
    nbs[zh] = named[:PAIR] | (named[PAIR:] << 16)
    widen(x, zl, 0, c)
    widen(x, zl, 1, c)
    taken(x, zl)
    go(1, x, zl, 1, right)
    go(2, x, zl, 0, left)
    go(5, x, zl, 1, over)
    loads[2].wait()
    loads[3].wait()
    loads[4].wait()
    for d in range(1, NY):
        remote(wf.at[f_id], wf.at[f_id], s_w, r_w, dev(d, 0, 0, 0)).start()
    remote(wf.at[f_id], wf.at[f_id], s_f, r_f, partner).start()

    lax.fori_loop(0, TGT // 8, fetch_own, 0)
    mates[...] = own[...].astype(BF).reshape(NY, SHARE, WIDE)
    theirs[y] = mates[y]
    for e in range(1, NY):
        remote(mates.at[(y + e) % NY], theirs.at[y], s_o, r_o, dev(e, 0, 0, 0)).start()

    come(0, xl, zl, 0)
    go(6, xl, zl, 0, right)
    go(11, xl, zl, 0, over)
    come(3, xr, zl, 1)
    go(7, xr, zl, 1, left)
    go(12, xr, zl, 1, over)
    come(4, x, zo, 0)
    go(8, x, zo, 0, dev(0, 0, 2, 0))
    go(10, x, zo, 0, left)
    pass_on(xl, zl, 0)
    pass_on(xr, zl, 1)
    pass_on(x, zo, 0)
    for d in range(1, NZG):
        remote(nbs.at[zh], nbs.at[zh], s_n.at[d], r_n.at[d], dev(0, 0, 0, 2 * d)).start()
    widen(xl, zl, 0, c)
    widen(xr, zl, 1, c)
    come(1, xl, zl, 1)
    go(13, xl, zl, 1, over)
    come(5, x, zo, 1)
    go(9, x, zo, 1, dev(0, 0, 2, 0))
    come(2, xr, zl, 0)
    pass_on(xl, zl, 1)
    pass_on(xr, zl, 0)
    pass_on(x, zo, 1)
    widen(x, zo, 0, c)
    widen(xl, zl, 1, c)
    widen(xr, zl, 0, c)
    widen(x, zo, 1, c)
    come(6, far, zl, 0)
    pass_on(far, zl, 0)
    come(7, far, zl, 1)
    pass_on(far, zl, 1)
    widen(far, zl, 0, c)
    widen(far, zl, 1, c)

    for d in range(1, NZG):
        at = (zh + NZG - d) % NZG
        arrived(nbs.at[at], r_n.at[d])
    for g in range(NZG):
        words = nbs[g]
        for h, n in enumerate((words & 0xFFFF, (words >> 16) & 0xFFFF)):
            part_of = n >> 11
            inside = ((part_of & 7) >> 1) == zh
            row = ((((part_of >> 3) << 1) | (part_of & 1)) << 11) | (n & (ROWS - 1))
            lists[g, h * PAIR : (h + 1) * PAIR, :] = jnp.where(inside, row, TAB)
    to_scalar = [
        pltpu.make_async_copy(lists.at[g, f], idx.at[pl.ds((g * FAN + f) * TGT, TGT)], s_idx)
        for g in range(NZG)
        for f in range(FAN)
    ]
    for copy in to_scalar:
        copy.start()
    rest = ((11, xl, 0), (12, xr, 1), (10, xr, 0), (8, far, 0), (13, xl, 1), (9, far, 1))
    for m, i, h in rest:
        come(m, i, zo, h)
        pass_on(i, zo, h)
    for m, i, h in rest:
        widen(i, zo, h, c)
    for i, zz in ((xl, zl), (xr, zl), (x, zo), (far, zl), (xr, zo), (xl, zo), (far, zo)):
        taken(i, zz)
    wide[pl.ds(TAB, 8), :] = jnp.zeros((8, WIDE), F32)
    pltpu.make_async_copy(idx, idx, s_idx).wait()

    def total_of(g, b, s):
        start = g * (FAN * TGT) + b * SHARE + s * RB

        def some(k, _):
            first = start + k * AT_ONCE
            for u in range(AT_ONCE):
                total = None
                for f in range(FAN):
                    skip = f * TGT + u
                    row = wide[pl.ds(idx.at[pl.ds(skip, LISTS - skip)][first], 1), :]
                    total = row if total is None else total + row
                own[pl.ds(k * AT_ONCE + u, 1), :] = total
            return 0

        lax.fori_loop(0, RB // AT_ONCE, some, 0)

    def plane(s, d):
        g = (zh + d) % NZG

        def one(e, _):
            total_of(g, (y + e) % NY, s)
            stage[e, d - 1] = own[pl.ds(0, RB), :].astype(BF)
            remote(stage.at[e, d - 1], pin.at[e, d - 1], s_p, r_p.at[e], dev(0, 0, 0, 2 * d)).start()
            return 0

        lax.fori_loop(0, NY, one, 0)

    def finish(s, e):
        b = (y + e) % NY
        total_of(zh, b, s)
        total = own[pl.ds(0, RB), :]
        arrived(pin.at[e], r_p.at[e])
        for d in range(NZG - 1):
            total = total + pin[e, d].astype(F32)
        means[s, b] = (total * (1.0 / FAN)).astype(BF)

    def home_plane(s):
        def one(e, _):
            finish(s, e)
            remote(means.at[s, (y + e) % NY], mine.at[s, y], s_m, r_m, dev(e, 0, 0, 0)).start()
            return 0

        lax.fori_loop(1, NY, one, 0)
        finish(s, 0)
        mine[s, y] = means[s, y]

    def activate(s):
        pre = jnp.zeros((RB, HID), F32)
        for b in range(NY):
            w_own = jnp.concatenate([wf[2 * b, 0], wf[2 * b + 1, 0]], axis=0)
            pre = pre + jnp.dot(theirs[b, s * RB : (s + 1) * RB, :], w_own, preferred_element_type=F32)
        for e in range(NY):
            src = (y + NY - e) % NY
            w_mean = jnp.concatenate([wf[2 * src, 1], wf[2 * src + 1, 1]], axis=0)
            if e == 0:
                arrived(mine.at[s, pl.ds(0, NY - 1)], r_m)
            pre = pre + jnp.dot(mine[s, src], w_mean, preferred_element_type=F32)
        square = pre * pre
        th = jnp.tanh(ROOT * (pre + 0.044715 * (square * pre)))
        half = 0.5 * (1.0 + th)
        dydx = half + 0.5 * pre * (1.0 - th * th) * (ROOT * (1.0 + 3.0 * 0.044715 * square))
        slopes[s, y] = (my_cot[s * RB : (s + 1) * RB, :].astype(F32) * dydx).astype(BF)
        for e in range(1, NY):
            remote(slopes.at[s, y], slopes.at[s, y], s_s, r_s, dev(e, 0, 0, 0)).start()
        hidden[s * RB : (s + 1) * RB, :] = (pre * half).astype(BF)

    def grads(s):
        mates_turned = jnp.transpose(mates[:, s * RB : (s + 1) * RB, :].reshape(NY * RB, WIDE))
        means_turned = jnp.transpose(means[s].reshape(NY * RB, WIDE))
        arrived(slopes.at[s, pl.ds(0, NY - 1)], r_s)
        slope = slopes[s].reshape(NY * RB, HID)
        return [jnp.dot(t, slope, preferred_element_type=F32) for t in (mates_turned, means_turned)]

    plane(0, 2)
    plane(0, 1)
    arrived(wf.at[pl.ds(0, NY - 1)], r_w)
    for d in range(1, NY):
        at = ((y + NY - d) % NY) * 2 + c
        remote(wf.at[at], wf.at[at], s_f, r_f, partner).start()
    plane(0, 3)
    home_plane(0)
    arrived(wf.at[pl.ds(0, NY)], r_f)
    arrived(theirs.at[pl.ds(0, NY - 1)], r_o)
    activate(0)
    both = grads(0)

    for p in range(2):
        for q in range(NX):
            for w in range(2):
                at = p * COLS + q * QROW
                gsend[p * NX + q, w] = both[w][at : at + QROW].astype(BF)
    hops = [(dc, dx) for dx in range(NX) for dc in range(2) if dc or dx]
    for n, (dc, dx) in enumerate(hops):
        core = 1 - c if dc else c
        remote(gsend.at[core * NX + (x + dx) % NX], gx.at[n], s_gx, r_gx, dev(0, dc, dx, 0)).start()
    total = gsend[c * NX + x].astype(F32)
    arrived(gx, r_gx)
    for n in range(len(hops)):
        total = total + gx[n].astype(F32)
    gz[z] = total.astype(BF)
    for d in range(1, NZ):
        remote(gz.at[z], gz.at[z], s_gz, r_gz, dev(0, 0, 0, d)).start()
    arrived(gz.at[pl.ds(0, NZ - 1)], r_gz)
    total = gz[0].astype(F32)
    for d in range(1, NZ):
        total = total + gz[d].astype(F32)
    gq[x] = total
    for d in range(1, NX):
        remote(gq.at[x], gq.at[x], s_gq, r_gq, dev(0, 0, d, 0)).start()
    arrived(gq.at[pl.ds(0, NX - 1)], r_gq)
    for q in range(NX):
        gself[q * QROW : (q + 1) * QROW, :] = gq[q, 0]
        gneigh[q * QROW : (q + 1) * QROW, :] = gq[q, 1]

    left_here(feat.at[:, pl.ds(give, HALF)], s_x)
    for m in range(7):
        left_here(tab.at[home, c], s_t.at[m])
    for m in range(GROUP):
        left_here(tab.at[home, c], s_h.at[m])
    for d in range(1, NZG):
        left_here(nbs.at[zh], s_n.at[d])
    left_here(wf.at[pl.ds(0, NY - 1)], s_w)
    left_here(theirs.at[pl.ds(0, NY - 1)], s_o)
    left_here(wf.at[pl.ds(0, NY)], s_f)

    left_here(stage, s_p)
    left_here(mine.at[0, pl.ds(0, NY - 1)], s_m)
    left_here(slopes.at[0, pl.ds(0, NY - 1)], s_s)
    left_here(gx, s_gx)
    left_here(gz.at[pl.ds(0, NZ - 1)], s_gz)
    left_here(gq.at[pl.ds(0, NX - 1)], s_gq)


def hand_over(a, b, c, out_a, out_b, out_c):
    out_a[...] = a[...]
    out_b[...] = b[...]
    out_c[...] = c[...]


VMEM = pl.BlockSpec(memory_space=pltpu.VMEM)
SMEM = pl.BlockSpec(memory_space=pltpu.SMEM)
HBM = pl.BlockSpec(memory_space=pl.ANY)


def sems(*counts):
    return [pltpu.SemaphoreType.DMA((n,)) if n else pltpu.SemaphoreType.DMA for n in counts for _ in range(2)]


def on_device(features, self_rows, neighbours, w_self, w_neigh, cotangent):
    shape = jax.ShapeDtypeStruct
    outs = [shape((SHARE, HID), BF), shape((COLS, HID), F32), shape((COLS, HID), F32)]
    got = pl.pallas_call(
        kernel,
        out_shape=outs,
        in_specs=[HBM, HBM, SMEM, HBM, HBM, HBM],
        out_specs=[VMEM] * 3,
        scratch_shapes=[
            pltpu.VMEM((FAN, 2 * TGT), I32),
            pltpu.VMEM((SHARE, HID), BF),
            pltpu.VMEM((2, COLS, HALF), BF),
            pltpu.VMEM((GROUP, 2, HALF, WIDE), BF),
            pltpu.VMEM((TAB + 8, WIDE), F32),
            pltpu.VMEM((NZG, PAIR, TGT), I32),
            pltpu.VMEM((NZG, FAN, TGT), I32),
            pltpu.SMEM((LISTS,), I32),
            pltpu.VMEM((2 * NY, 2, COLS, HID), BF),
            pltpu.VMEM((TGT, WIDE), F32),
            pltpu.VMEM((NY, SHARE, WIDE), BF),
            pltpu.VMEM((NY, NZG - 1, RB, WIDE), BF),
            pltpu.VMEM((NY, NZG - 1, RB, WIDE), BF),
            pltpu.VMEM((NS, NY, RB, WIDE), BF),
            pltpu.VMEM((NS, NY, RB, HID), BF),
            pltpu.VMEM((NS, NY, RB, WIDE), BF),
            pltpu.VMEM((NY, SHARE, WIDE), BF),
            pltpu.VMEM((2 * NX, 2, QROW, HID), BF),
            pltpu.VMEM((2 * NX - 1, 2, QROW, HID), BF),
            pltpu.VMEM((NZ, 2, QROW, HID), BF),
            pltpu.VMEM((NX, 2, QROW, HID), F32),
            *sems(0),
            *(pltpu.SemaphoreType.DMA((n,)) for n in (7, 14, GROUP, GROUP, NZG, NZG)),
            *sems(0, 0, 0),
            pltpu.SemaphoreType.DMA,
            pltpu.SemaphoreType.DMA((NY,)),
            *sems(0, 0, 0, 0, 0),
            pltpu.SemaphoreType.DMA,
            pltpu.SemaphoreType.DMA((5,)),
        ],
        compiler_params=pltpu.CompilerParams(collective_id=0, has_side_effects=True, vmem_limit_bytes=56 * 2**20),
        name="layer",
    )(features.T, neighbours, self_rows, w_self, w_neigh, cotangent)
    return tuple(
        pl.pallas_call(hand_over, out_shape=outs, in_specs=[VMEM] * 3, out_specs=[VMEM] * 3, name="results")(*got)
    )


def solution(mesh):
    return jax.shard_map(
        on_device,
        mesh=mesh,
        in_specs=(
            P("node", "feat"),
            P("node"),
            P(None, "node"),
            P("feat", None),
            P("feat", None),
            P("node", None),
        ),
        out_specs=(P(("node", "feat"), None), P("feat", None), P("feat", None)),
        check_vma=False,
    )
```

time: 88.4 us -> 85.3 us (0.965)
  Pallas kernels: 87.6 us -> 83.9 us
    pallas_call x1, Pallas kernels: 86 us -> 82.4 us  [on_device(): pl.pallas_call(kernel, out_shape=outs, in_specs=[HBM, HBM, SMEM, HBM, HBM...]
where the time goes in v4:
time: 85.3 us; the launch traced here: 84.6 us
  Pallas kernels  83.9 us (98%)
    pallas_call x1, Pallas kernels, on_device(): pl.pallas_call(kernel, out_shape=outs, in_specs=[HBM, HBM, SMEM, HBM, HBM...  82.4 us

profile of v4, /device:TPU:1, one launch (start us, length us, event | category | flops | bytes accessed | tf_op | source)
XLA Modules:
  0.0 84.6 jit_solution(11393203654123215442)
XLA Ops:
  0.6 82.4 %layer.1 = (bf16[64,256]{1,0:T(8,128)(2,1)}, f32[64,256]{1,0:T(8,128)}, f32[64,256]{1,0:T(8,128)}) custom-call(bf16[64,2048]{1,0:T(8,128)(2,1)} %bitcast.1, s32[10,1024]{1,0:T(8,128)} %nb.1, s32[1024]{0:T(1024)} %rows.1, bf16[64,256]{1,0:T(8,128)(2,1)} %ws.1, bf16[64,256]{1,0:T(8,128)(2,1)} %wn.1, bf16[1024,256]{1,0:T(8,128)(2,1)} %cot.1), custom_call_target="tpu_custom_call" | custom-call | tf_op jit(solution)/shard_map/layer/pallas_call | solution.py:394
  83.0 1.6 %results.1 = (bf16[64,256]{1,0:T(8,128)(2,1)}, f32[64,256]{1,0:T(8,128)}, f32[64,256]{1,0:T(8,128)}) custom-call(bf16[64,256]{1,0:T(8,128)(2,1)} %get-tuple-element.6.a, f32[64,256]{1,0:T(8,128)} %get-tuple-element.7.b, f32[64,256]{1,0:T(8,128)} %get-tuple-element.8.c), custom_call_target="tpu_custom_call" | custom-call | tf_op jit(solution)/shard_map/results/pallas_call | solution.py:434

commit v5 on v4

--- a/solution.py
+++ b/solution.py
@@ -65,7 +65,7 @@
     friends = [partner]
     friends += [dev(0, 0, 0, d) for d in range(1, NZ)]
     friends += [dev(0, dc, d, 0) for d in range(1, NX) for dc in range(2)]
-    friends += [dev(e, 0, 0, 2 * d) for d in range(NZG) for e in range(1, NY)]
+    friends += [dev(e, 0, 0, 0) for e in range(1, NY)]
     for to in friends:
         pl.semaphore_signal(barrier, inc=1, device_id=to, device_id_type=MESH)
 

time: 85.3 us -> 82.8 us (0.971)
  Pallas kernels: 83.9 us -> 81.6 us
    pallas_call x1, Pallas kernels: 82.4 us -> 80 us  [on_device(): pl.pallas_call(kernel, out_shape=outs, in_specs=[HBM, HBM, SMEM, HBM, HBM...]
where the time goes in v5:
time: 82.8 us; the launch traced here: 82.2 us
  Pallas kernels  81.6 us (99%)
    pallas_call x1, Pallas kernels, on_device(): pl.pallas_call(kernel, out_shape=outs, in_specs=[HBM, HBM, SMEM, HBM, HBM...  80 us

profile of v5, /device:TPU:1, one launch (start us, length us, event | category | flops | bytes accessed | tf_op | source)
XLA Modules:
  0.0 82.2 jit_solution(18080027754912492341)
XLA Ops:
  0.6 80.0 %layer.1 = (bf16[64,256]{1,0:T(8,128)(2,1)}, f32[64,256]{1,0:T(8,128)}, f32[64,256]{1,0:T(8,128)}) custom-call(bf16[64,2048]{1,0:T(8,128)(2,1)} %bitcast.1, s32[10,1024]{1,0:T(8,128)} %nb.1, s32[1024]{0:T(1024)} %rows.1, bf16[64,256]{1,0:T(8,128)(2,1)} %ws.1, bf16[64,256]{1,0:T(8,128)(2,1)} %wn.1, bf16[1024,256]{1,0:T(8,128)(2,1)} %cot.1), custom_call_target="tpu_custom_call" | custom-call | tf_op jit(solution)/shard_map/layer/pallas_call | solution.py:394
  80.7 1.6 %results.1 = (bf16[64,256]{1,0:T(8,128)(2,1)}, f32[64,256]{1,0:T(8,128)}, f32[64,256]{1,0:T(8,128)}) custom-call(bf16[64,256]{1,0:T(8,128)(2,1)} %get-tuple-element.6.a, f32[64,256]{1,0:T(8,128)} %get-tuple-element.7.b, f32[64,256]{1,0:T(8,128)} %get-tuple-element.8.c), custom_call_target="tpu_custom_call" | custom-call | tf_op jit(solution)/shard_map/results/pallas_call | solution.py:434

commit v6 on v5

--- a/solution.py
+++ b/solution.py
@@ -288,15 +288,15 @@
 
     def activate(s):
         pre = jnp.zeros((RB, HID), F32)
-        for b in range(NY):
-            w_own = jnp.concatenate([wf[2 * b, 0], wf[2 * b + 1, 0]], axis=0)
-            pre = pre + jnp.dot(theirs[b, s * RB : (s + 1) * RB, :], w_own, preferred_element_type=F32)
-        for e in range(NY):
-            src = (y + NY - e) % NY
-            w_mean = jnp.concatenate([wf[2 * src, 1], wf[2 * src + 1, 1]], axis=0)
-            if e == 0:
-                arrived(mine.at[s, pl.ds(0, NY - 1)], r_m)
-            pre = pre + jnp.dot(mine[s, src], w_mean, preferred_element_type=F32)
+        for b in range(0, NY, 2):
+            w_own = jnp.concatenate([wf[2 * b + k, 0] for k in range(4)], axis=0)
+            got = jnp.concatenate([theirs[b], theirs[b + 1]], axis=1)
+            pre = pre + jnp.dot(got, w_own, preferred_element_type=F32)
+        arrived(mine.at[s, pl.ds(0, NY - 1)], r_m)
+        for b in range(0, NY, 2):
+            w_mean = jnp.concatenate([wf[2 * b + k, 1] for k in range(4)], axis=0)
+            got = jnp.concatenate([mine[s, b], mine[s, b + 1]], axis=1)
+            pre = pre + jnp.dot(got, w_mean, preferred_element_type=F32)
         square = pre * pre
         th = jnp.tanh(ROOT * (pre + 0.044715 * (square * pre)))
         half = 0.5 * (1.0 + th)

time: 82.8 us -> 82.8 us (level)
  no operation moved by 1% of the time
where the time goes in v6:
time: 82.8 us; the launch traced here: 82.2 us
  Pallas kernels  81.6 us (99%)
    pallas_call x1, Pallas kernels, on_device(): pl.pallas_call(kernel, out_shape=outs, in_specs=[HBM, HBM, SMEM, HBM, HBM...  80 us

profile of v6, /device:TPU:1, one launch (start us, length us, event | category | flops | bytes accessed | tf_op | source)
XLA Modules:
  0.0 82.2 jit_solution(3307927151581086059)
XLA Ops:
  0.6 80.0 %layer.1 = (bf16[64,256]{1,0:T(8,128)(2,1)}, f32[64,256]{1,0:T(8,128)}, f32[64,256]{1,0:T(8,128)}) custom-call(bf16[64,2048]{1,0:T(8,128)(2,1)} %bitcast.1, s32[10,1024]{1,0:T(8,128)} %nb.1, s32[1024]{0:T(1024)} %rows.1, bf16[64,256]{1,0:T(8,128)(2,1)} %ws.1, bf16[64,256]{1,0:T(8,128)(2,1)} %wn.1, bf16[1024,256]{1,0:T(8,128)(2,1)} %cot.1), custom_call_target="tpu_custom_call" | custom-call | tf_op jit(solution)/shard_map/layer/pallas_call | solution.py:394
  80.7 1.6 %results.1 = (bf16[64,256]{1,0:T(8,128)(2,1)}, f32[64,256]{1,0:T(8,128)}, f32[64,256]{1,0:T(8,128)}) custom-call(bf16[64,256]{1,0:T(8,128)(2,1)} %get-tuple-element.6.a, f32[64,256]{1,0:T(8,128)} %get-tuple-element.7.b, f32[64,256]{1,0:T(8,128)} %get-tuple-element.8.c), custom_call_target="tpu_custom_call" | custom-call | tf_op jit(solution)/shard_map/results/pallas_call | solution.py:434
